TPU v7x, 32 devices: a whole 2x2x4 slice. The times are simulated.
32 devices in a mesh: dp: 4 (over y, core), ctx: 8 (over z, x).
Axes of the slice: x: 2, y: 2, z: 4, core: 2. Of those that a mesh axis runs over, the one named last changes fastest.
Arguments:
- tokens: bfloat16 [8, 1024, 768], P('dp', 'ctx'), may hold values from -6 to 6
- ln1_gain: bfloat16 [768], P(('dp', 'ctx')), may hold values from 0.5 to 1.5
- ln1_bias: bfloat16 [768], P(('dp', 'ctx')), may hold values from -1.5 to 1.5
- w_qkv: bfloat16 [768, 2304], P(('dp', 'ctx')), may hold values from -0.3125 to 0.3125
- b_qv: bfloat16 [1536], P(('dp', 'ctx')), may hold values from -1.5 to 1.5
- w_proj: bfloat16 [768, 768], P(('dp', 'ctx')), may hold values from -1.75 to 1.75
- b_proj: bfloat16 [768], P(('dp', 'ctx')), may hold values from -4 to 4
- ln2_gain: bfloat16 [768], P(('dp', 'ctx')), may hold values from 0.5 to 1.5
- ln2_bias: bfloat16 [768], P(('dp', 'ctx')), may hold values from -1.5 to 1.5
- w_fc: bfloat16 [768, 3072], P(('dp', 'ctx')), may hold values from -0.21875 to 0.21875
- b_fc: bfloat16 [3072], P(('dp', 'ctx')), may hold values from -1.5 to 1.5
- w_out: bfloat16 [3072, 768], P(('dp', 'ctx')), may hold values from -0.109375 to 0.109375
- b_out: bfloat16 [768], P(('dp', 'ctx')), may hold values from -4 to 4
- cotangent: bfloat16 [8, 1024, 768], P('dp', 'ctx'), may hold values from -6 to 6
Outputs:
- block_out: bfloat16 [8, 1024, 768], P('dp', 'ctx')
- grad_tokens: float32 [8, 1024, 768], P('dp', 'ctx')
- grad_ln1_gain: float32 [768], P(('dp', 'ctx'))
- grad_ln1_bias: float32 [768], P(('dp', 'ctx'))
- grad_w_qkv: float32 [768, 2304], P(('dp', 'ctx'))
- grad_b_qv: float32 [1536], P(('dp', 'ctx'))
- grad_w_proj: float32 [768, 768], P(('dp', 'ctx'))
- grad_b_proj: float32 [768], P(('dp', 'ctx'))
- grad_ln2_gain: float32 [768], P(('dp', 'ctx'))
- grad_ln2_bias: float32 [768], P(('dp', 'ctx'))
- grad_w_fc: float32 [768, 3072], P(('dp', 'ctx'))
- grad_b_fc: float32 [3072], P(('dp', 'ctx'))
- grad_w_out: float32 [3072, 768], P(('dp', 'ctx'))
- grad_b_out: float32 [768], P(('dp', 'ctx'))
All inputs are finite; a program needn't handle non-finite values.
Results may differ from a plain program's by a relative error of at most 0.035.
Values may be sent and summed in bfloat16 or wider, within the bound.
No kernel may reach another device: no remote copies, remote signals or barrier semaphores. Data moves between devices by JAX's collectives and lax.ppermute only.
A program may use at most 192 MiB of HBM per device.

v0:
```python
import math

import jax
import jax.numpy as jnp
from jax import lax
from jax.sharding import PartitionSpec as P

H = 12
HD = 64


EPS = 1e-05
NEG = -1e30


def layer_norm(values, gain_vec, bias_vec):
    average = jnp.mean(values, axis=-1, keepdims=True)
    centered = values - average
    variance = jnp.mean(centered * centered, axis=-1, keepdims=True)
    return centered * lax.rsqrt(variance + EPS) * gain_vec + bias_vec


def gelu_tanh(values):
    return jax.nn.gelu(values, approximate=True)


def outer_sum(left, right):
    return lax.dot_general(
        left, right, (((0,), (0,)), ((), ())), preferred_element_type=jnp.float32
    )


def back_through(grad_rows, weight_mat):
    return lax.dot_general(
        grad_rows, weight_mat, (((1,), (1,)), ((), ())), preferred_element_type=jnp.float32
    )


def split_heads(flat_rows):
    return flat_rows.reshape(flat_rows.shape[0], flat_rows.shape[1], H, HD)


def attend_block(query_rows, key_rows, value_rows, query_pos, key_pos, running):
    factor = 1.0 / math.sqrt(HD)
    scores = (
        jnp.einsum("sqhd,skhd->shqk", query_rows, key_rows, preferred_element_type=jnp.float32)
        * factor
    )
    visible = key_pos[None, :] <= query_pos[:, None]
    scores = jnp.where(visible, scores, NEG)
    run_max, run_sum, run_acc = running
    new_max = jnp.maximum(run_max, jnp.max(scores, axis=-1))
    weights = jnp.where(visible, jnp.exp(scores - new_max[..., None]), 0.0)
    new_sum = jnp.sum(weights, axis=-1)
    added = jnp.einsum(
        "shqk,skhd->shqd",
        weights.astype(jnp.bfloat16),
        value_rows,
        preferred_element_type=jnp.float32,
    )
    return (new_max, new_sum, added)


def attend_grad(
    query_rows, grad_heads, log_total, delta_rows, key_rows, value_rows, query_pos, key_pos
):
    factor = 1.0 / math.sqrt(HD)
    scores = (
        jnp.einsum("sqhd,skhd->shqk", query_rows, key_rows, preferred_element_type=jnp.float32)
        * factor
    )
    visible = key_pos[None, :] <= query_pos[:, None]
    probs = jnp.where(visible, jnp.exp(scores - log_total[..., None]), 0.0)
    grad_values = jnp.einsum(
        "shqk,sqhd->skhd",
        probs.astype(jnp.bfloat16),
        grad_heads,
        preferred_element_type=jnp.float32,
    )
    grad_probs = jnp.einsum(
        "sqhd,skhd->shqk", grad_heads, value_rows, preferred_element_type=jnp.float32
    )
    grad_scores = (probs * (grad_probs - delta_rows[..., None])).astype(jnp.bfloat16)
    grad_query = (
        jnp.einsum("shqk,skhd->sqhd", grad_scores, key_rows, preferred_element_type=jnp.float32)
        * factor
    )
    grad_keys = (
        jnp.einsum("shqk,sqhd->skhd", grad_scores, query_rows, preferred_element_type=jnp.float32)
        * factor
    )
    return (grad_query, grad_keys, grad_values)


def body(
    tokens,
    ln1_gain,
    ln1_bias,
    w_qkv,
    b_qv,
    w_proj,
    b_proj,
    ln2_gain,
    ln2_bias,
    w_fc,
    b_fc,
    w_out,
    b_out,
    cotangent,
):
    gathered = (
        lax.all_gather(ln1_gain, ("dp", "ctx"), axis=0, tiled=True),
        lax.all_gather(ln1_bias, ("dp", "ctx"), axis=0, tiled=True),
        lax.all_gather(w_qkv, ("dp", "ctx"), axis=0, tiled=True),
        lax.all_gather(b_qv, ("dp", "ctx"), axis=0, tiled=True),
        lax.all_gather(w_proj, ("dp", "ctx"), axis=0, tiled=True),
        lax.all_gather(b_proj, ("dp", "ctx"), axis=0, tiled=True),
        lax.all_gather(ln2_gain, ("dp", "ctx"), axis=0, tiled=True),
        lax.all_gather(ln2_bias, ("dp", "ctx"), axis=0, tiled=True),
        lax.all_gather(w_fc, ("dp", "ctx"), axis=0, tiled=True),
        lax.all_gather(b_fc, ("dp", "ctx"), axis=0, tiled=True),
        lax.all_gather(w_out, ("dp", "ctx"), axis=0, tiled=True),
        lax.all_gather(b_out, ("dp", "ctx"), axis=0, tiled=True),
    )
    (
        gain_one,
        bias_one,
        qkv_weight,
        qkv_bias,
        proj_weight,
        proj_bias,
        gain_two,
        bias_two,
        fc_weight,
        fc_bias,
        out_weight,
        out_bias,
    ) = gathered
    count_seq, group_len, model_width = tokens.shape
    rows_total = count_seq * group_len
    query_pos = lax.axis_index("ctx") * group_len + jnp.arange(group_len, dtype=jnp.int32)
    inputs = tokens.astype(jnp.float32).reshape(rows_total, model_width)
    normed_one, pull_one = jax.vjp(
        layer_norm, inputs, gain_one.astype(jnp.float32), bias_one.astype(jnp.float32)
    )
    normed_low = normed_one.astype(jnp.bfloat16)
    qkv_bias32 = qkv_bias.astype(jnp.float32)
    bias_full = jnp.concatenate(
        [qkv_bias32[:model_width], jnp.zeros((model_width,), jnp.float32), qkv_bias32[model_width:]]
    )
    qkv_low = (
        jnp.dot(normed_low, qkv_weight, preferred_element_type=jnp.float32) + bias_full
    ).astype(jnp.bfloat16)
    query_flat = qkv_low[:, :model_width].reshape(count_seq, group_len, model_width)
    query_rows = split_heads(query_flat)
    key_value = qkv_low[:, model_width:].reshape(count_seq, group_len, 2 * model_width)
    initial = (
        jnp.full((count_seq, H, group_len), NEG, jnp.float32),
        jnp.zeros((count_seq, H, group_len), jnp.float32),
        jnp.zeros((count_seq, H, group_len, HD), jnp.float32),
    )
    remote = lax.all_gather(key_value, "ctx", axis=1, tiled=True)
    rows_here = remote.shape[1]
    key_pos = jnp.arange(rows_here, dtype=jnp.int32)
    key_rows = split_heads(remote[:, :, :model_width])
    value_rows = split_heads(remote[:, :, model_width:])
    run_max, run_sum, run_acc = attend_block(
        query_rows, key_rows, value_rows, query_pos, key_pos, initial
    )
    attended = run_acc / run_sum[..., None]
    log_total = run_max + jnp.log(run_sum)
    merged_low = (
        attended.transpose(0, 2, 1, 3).reshape(rows_total, model_width).astype(jnp.bfloat16)
    )
    middle = (
        inputs
        + jnp.dot(merged_low, proj_weight, preferred_element_type=jnp.float32)
        + proj_bias.astype(jnp.float32)
    )
    normed_two, pull_two = jax.vjp(
        layer_norm, middle, gain_two.astype(jnp.float32), bias_two.astype(jnp.float32)
    )
    normed_two_low = normed_two.astype(jnp.bfloat16)
    pre_act = jnp.dot(
        normed_two_low, fc_weight, preferred_element_type=jnp.float32
    ) + fc_bias.astype(jnp.float32)
    activated, gelu_pull = jax.vjp(gelu_tanh, pre_act)
    activated_low = activated.astype(jnp.bfloat16)
    feed_out = jnp.dot(
        activated_low, out_weight, preferred_element_type=jnp.float32
    ) + out_bias.astype(jnp.float32)
    result = (middle + feed_out).astype(jnp.bfloat16).reshape(count_seq, group_len, model_width)
    regathered = (
        lax.all_gather(ln1_gain, ("dp", "ctx"), axis=0, tiled=True),
        lax.all_gather(ln1_bias, ("dp", "ctx"), axis=0, tiled=True),
        lax.all_gather(w_qkv, ("dp", "ctx"), axis=0, tiled=True),
        lax.all_gather(b_qv, ("dp", "ctx"), axis=0, tiled=True),
        lax.all_gather(w_proj, ("dp", "ctx"), axis=0, tiled=True),
        lax.all_gather(b_proj, ("dp", "ctx"), axis=0, tiled=True),
        lax.all_gather(ln2_gain, ("dp", "ctx"), axis=0, tiled=True),
        lax.all_gather(ln2_bias, ("dp", "ctx"), axis=0, tiled=True),
        lax.all_gather(w_fc, ("dp", "ctx"), axis=0, tiled=True),
        lax.all_gather(b_fc, ("dp", "ctx"), axis=0, tiled=True),
        lax.all_gather(w_out, ("dp", "ctx"), axis=0, tiled=True),
        lax.all_gather(b_out, ("dp", "ctx"), axis=0, tiled=True),
    )
    qkv_weight = regathered[2]
    proj_weight = regathered[4]
    fc_weight = regathered[8]
    out_weight = regathered[10]
    grad_top = cotangent.reshape(rows_total, model_width)
    grad_top32 = grad_top.astype(jnp.float32)
    grad_out_bias = jnp.sum(grad_top32, axis=0)
    grad_out_weight = outer_sum(activated_low, grad_top)
    grad_act = back_through(grad_top, out_weight)
    grad_pre = gelu_pull(grad_act)[0].astype(jnp.bfloat16)
    grad_fc_bias = jnp.sum(grad_pre.astype(jnp.float32), axis=0)
    grad_fc_weight = outer_sum(normed_two_low, grad_pre)
    grad_normed_two = back_through(grad_pre, fc_weight)
    grad_middle_ln, grad_gain_two, grad_bias_two = pull_two(grad_normed_two)
    grad_middle = grad_top32 + grad_middle_ln
    grad_branch = grad_middle.astype(jnp.bfloat16)
    grad_proj_bias = jnp.sum(grad_branch.astype(jnp.float32), axis=0)
    grad_proj_weight = outer_sum(merged_low, grad_branch)
    grad_merged = back_through(grad_branch, proj_weight).astype(jnp.bfloat16)
    grad_flat = grad_merged.reshape(count_seq, group_len, model_width)
    grad_heads = split_heads(grad_flat)
    delta_rows = jnp.einsum("sqhd,shqd->shq", grad_heads.astype(jnp.float32), attended)
    remote = lax.all_gather(key_value, "ctx", axis=1, tiled=True)
    rows_here = remote.shape[1]
    key_pos = jnp.arange(rows_here, dtype=jnp.int32)
    part_query, part_keys, part_values = attend_grad(
        query_rows,
        grad_heads,
        log_total,
        delta_rows,
        split_heads(remote[:, :, :model_width]),
        split_heads(remote[:, :, model_width:]),
        query_pos,
        key_pos,
    )
    joined = jnp.concatenate(
        [
            part_keys.reshape(count_seq, rows_here, model_width),
            part_values.reshape(count_seq, rows_here, model_width),
        ],
        axis=2,
    )
    grad_kv_all = joined
    grad_query, grad_kv_all = (part_query, grad_kv_all)
    grad_kv = lax.psum_scatter(
        grad_kv_all.astype(jnp.bfloat16), "ctx", scatter_dimension=1, tiled=True
    ).astype(jnp.float32)
    grad_query_flat = grad_query.reshape(count_seq, group_len, model_width)
    grad_qkv = jnp.concatenate(
        [
            grad_query_flat.reshape(rows_total, model_width),
            grad_kv.reshape(rows_total, 2 * model_width),
        ],
        axis=1,
    ).astype(jnp.bfloat16)
    column_sums = jnp.sum(grad_qkv.astype(jnp.float32), axis=0)
    grad_qkv_bias = jnp.concatenate([column_sums[:model_width], column_sums[2 * model_width :]])
    grad_qkv_weight = outer_sum(normed_low, grad_qkv)
    grad_normed_one = back_through(grad_qkv, qkv_weight)
    grad_input_ln, grad_gain_one, grad_bias_one = pull_one(grad_normed_one)
    grad_input = (grad_middle + grad_input_ln).reshape(count_seq, group_len, model_width)
    gradients = (
        lax.psum_scatter(grad_gain_one, ("dp", "ctx"), scatter_dimension=0, tiled=True),
        lax.psum_scatter(grad_bias_one, ("dp", "ctx"), scatter_dimension=0, tiled=True),
        lax.psum_scatter(grad_qkv_weight, ("dp", "ctx"), scatter_dimension=0, tiled=True),
        lax.psum_scatter(grad_qkv_bias, ("dp", "ctx"), scatter_dimension=0, tiled=True),
        lax.psum_scatter(grad_proj_weight, ("dp", "ctx"), scatter_dimension=0, tiled=True),
        lax.psum_scatter(grad_proj_bias, ("dp", "ctx"), scatter_dimension=0, tiled=True),
        lax.psum_scatter(grad_gain_two, ("dp", "ctx"), scatter_dimension=0, tiled=True),
        lax.psum_scatter(grad_bias_two, ("dp", "ctx"), scatter_dimension=0, tiled=True),
        lax.psum_scatter(grad_fc_weight, ("dp", "ctx"), scatter_dimension=0, tiled=True),
        lax.psum_scatter(grad_fc_bias, ("dp", "ctx"), scatter_dimension=0, tiled=True),
        lax.psum_scatter(grad_out_weight, ("dp", "ctx"), scatter_dimension=0, tiled=True),
        lax.psum_scatter(grad_out_bias, ("dp", "ctx"), scatter_dimension=0, tiled=True),
    )
    return (result, grad_input) + tuple(gradients)


def solution(mesh):
    placed = (
        P("dp", "ctx", None),
        P(("dp", "ctx")),
        P(("dp", "ctx")),
        P(("dp", "ctx"), None),
        P(("dp", "ctx")),
        P(("dp", "ctx"), None),
        P(("dp", "ctx")),
        P(("dp", "ctx")),
        P(("dp", "ctx")),
        P(("dp", "ctx"), None),
        P(("dp", "ctx")),
        P(("dp", "ctx"), None),
        P(("dp", "ctx")),
        P("dp", "ctx", None),
    )
    return jax.shard_map(
        body,
        mesh=mesh,
        in_specs=placed,
        out_specs=(
            P("dp", "ctx", None),
            P("dp", "ctx", None),
            P(("dp", "ctx")),
            P(("dp", "ctx")),
            P(("dp", "ctx"), None),
            P(("dp", "ctx")),
            P(("dp", "ctx"), None),
            P(("dp", "ctx")),
            P(("dp", "ctx")),
            P(("dp", "ctx")),
            P(("dp", "ctx"), None),
            P(("dp", "ctx")),
            P(("dp", "ctx"), None),
            P(("dp", "ctx")),
        ),
        check_vma=False,
    )
```

profile of v0, /device:TPU:0, one launch (start us, length us, event | category | flops | bytes accessed | tf_op | source)
XLA Modules:
  0.0 1057.0 jit_solution(1820861755903409341)
XLA Ops:
  15.4 42.6 %all-reduce.17 = (bf16[768]{0:T(1024)(128)(2,1)S(1)}, bf16[768]{0:T(1024)(128)(2,1)S(1)}, bf16[768]{0:T(1024)(128)(2,1)S(1)}, bf16[1536]{0:T(1024)(128)(2,1)S(1)...) all-reduce(bf16[768]{0:T(1024)(128)(2,1)S(1)} %dynamic-update-slice, ...), channel_id=1, replica_groups=mesh['dp'=4,'ctx'=8] {'dp','ctx'}, use_global_device_ids=true, to_apply=%add.3 | all-reduce | flops 9216 | bytes 36864
  58.0 1.1 convert_reduce_fusion.4
  59.2 1.2 multiply_reduce_fusion.6
  60.5 1.2 add_convert_fusion.1
  61.7 12.3 %all-gather.6.cloned.1.call-done = bf16[768,2304]{1,0:T(8,128)(2,1)} async-done(((bf16[24,2304]{1,0:T(8,128)(2,1)}), bf16[768,2304]{1,0:T(8,128)(2,1)}) %all-gather.6.cloned.1.call-update) | async-done | bytes 3538960 | tf_op jit(solution)/shard_map/all_gather | solution.py:114
  74.0 3.1 fusion.12
  77.1 0.9 slice.37
  81.6 57.9 %all-gather.14.cloned.1.call-done = bf16[3072,768]{1,0:T(8,128)(2,1)} async-done(((bf16[96,768]{1,0:T(8,128)(2,1)}), bf16[3072,768]{1,0:T(8,128)(2,1)}) %all-gather.14.cloned.1.call-update) | async-done | bytes 4718608 | tf_op jit(solution)/shard_map/all_gather | solution.py:122
  139.5 5.4 fusion.62
  144.9 95.2 %all-gather.8.cloned.1.call-done = bf16[2,1024,1536]{2,1,0:T(8,128)(2,1)} async-done(((bf16[2,128,1536]{2,1,0:T(8,128)(2,1)}), bf16[2,1024,1536]{2,1,0:T(8,128)(2,1)}) %all-gather.8.cloned.1.call-update) | async-done | bytes 6291472 | tf_op jit(solution)/shard_map/all_gather | solution.py:162
  240.1 5.9 fusion.58
  246.1 3.2 copy.48
  249.2 4.7 copy.50
  253.9 3.3 select_reduce_fusion
  257.3 4.0 fusion.1
  261.2 1.3 copy-done
  262.6 7.4 fusion.28
  270.0 1.2 copy.51
  271.1 24.2 %all-gather.10.cloned.1.call-done = bf16[768,768]{1,0:T(8,128)(2,1)} async-done(((bf16[24,768]{1,0:T(8,128)(2,1)}), bf16[768,768]{1,0:T(8,128)(2,1)}) %all-gather.10.cloned.1.call-update) | async-done | bytes 1179664 | tf_op jit(solution)/shard_map/all_gather | solution.py:116
  295.4 2.0 fusion.61
  300.3 60.5 %all-gather.12.cloned.1.call-done = bf16[768,3072]{1,0:T(8,128)(2,1)} async-done(((bf16[24,3072]{1,0:T(8,128)(2,1)}), bf16[768,3072]{1,0:T(8,128)(2,1)}) %all-gather.12.cloned.1.call-update) | async-done | bytes 4718608 | tf_op jit(solution)/shard_map/all_gather | solution.py:120
  360.8 9.5 convert_reduce_fusion
  370.4 2.2 multiply_reduce_fusion.1
  374.7 1.3 convolution_convert_fusion
  376.0 1.9 copy.52
  377.9 1.9 reshape_reshape.11
  379.7 2.2 bitcast_convert_fusion
  381.9 9.2 fusion.20
  391.1 4.7 copy.58
  395.9 1.5 multiply_reduce_fusion
  397.4 8.5 multiply_convert_fusion
  405.9 3.3 multiply_convert_fusion.1
  409.6 4.7 copy.57
  414.3 6.0 pad_maximum_fusion
  420.4 3.0 fusion.30
  423.5 6.9 fusion.52
  430.4 7.8 fusion.53
  438.5 5.1 fusion.27
  444.3 93.0 %reduce-scatter.6.cloned.1.call-done = bf16[2,128,1536]{2,1,0:T(8,128)(2,1)} async-done(((bf16[2,1024,1536]{2,1,0:T(8,128)(2,1)}), bf16[2,128,1536]{2,1,0:T(8,128)(2,1)}) %reduce-scatter.6.cloned.1.call-update) | async-done | bytes 786448 | tf_op jit(solution)/shard_map/reduce_scatter | solution.py:251
  537.3 5.3 fusion.40
  544.2 6.1 fusion.25
  550.6 1.7 fusion.54
  552.8 40.7 %all-reduce.16 = (f32[768]{0:T(1024)S(1)}, f32[768]{0:T(1024)S(1)}, f32[1536]{0:T(1024)S(1)}, f32[768]{0:T(1024)S(1)}, f32[768]{0:T(1024)S(1)}, /*index=5*/f32[7...) all-reduce(f32[768]{0:T(1024)S(1)} %get-tuple-element.16, ...), channel_id=3, replica_groups=mesh['dp'=4,'ctx'=8] {'dp','ctx'}, use_global_device_ids=true, to_apply=%region_12.13.clone | all-reduce | flops 9216 | bytes 73728
  598.2 1.9 add_add_fusion.2
  600.1 41.4 %reduce-scatter.10.cloned.1.call-done = f32[24,768]{1,0:T(8,128)} async-done(((f32[768,768]{1,0:T(8,128)}), f32[24,768]{1,0:T(8,128)}) %reduce-scatter.10.cloned.1.call-update) | async-done | bytes 73744 | tf_op jit(solution)/shard_map/reduce_scatter | solution.py:273
  641.5 142.0 %reduce-scatter.12.cloned.1.call-done = f32[24,3072]{1,0:T(8,128)} async-done(((f32[768,3072]{1,0:T(8,128)}), f32[24,3072]{1,0:T(8,128)}) %reduce-scatter.12.cloned.1.call-update) | async-done | bytes 294928 | tf_op jit(solution)/shard_map/reduce_scatter | solution.py:277
  783.6 141.3 %reduce-scatter.14.cloned.1.call-done = f32[96,768]{1,0:T(8,128)} async-done(((f32[3072,768]{1,0:T(8,128)}), f32[96,768]{1,0:T(8,128)}) %reduce-scatter.14.cloned.1.call-update) | async-done | bytes 294928 | tf_op jit(solution)/shard_map/reduce_scatter | solution.py:279
  924.8 125.1 %reduce-scatter.8.cloned.1.call-done = f32[24,2304]{1,0:T(8,128)} async-done(((f32[768,2304]{1,0:T(8,128)}), f32[24,2304]{1,0:T(8,128)}) %reduce-scatter.8.cloned.1.call-update) | async-done | bytes 221200 | tf_op jit(solution)/shard_map/reduce_scatter | solution.py:271
  (153 shorter events, 25.2 us)
Async XLA Ops:
  7.2 66.8 %all-gather.6.cloned.1.call-start = ((), (), s32[]{:S(2)}) async-start(), calls=%async_computation.5 | async-start | bytes 3649536 | tf_op jit(solution)/shard_map/all_gather | solution.py:114
  7.9 131.6 %all-gather.14.cloned.1.call-start = ((), (), s32[]{:S(2)}) async-start(), calls=%async_computation.9 | async-start | bytes 4866048 | tf_op jit(solution)/shard_map/all_gather | solution.py:122
  8.7 231.5 %all-gather.8.cloned.1.call-start = ((), (), s32[]{:S(2)}) async-start(), calls=%async_computation.6 | async-start | bytes 7077888 | tf_op jit(solution)/shard_map/all_gather | solution.py:162
  59.2 17.9 %copy-start.24 = (f32[256]{0:T(256)}, f32[256]{0:T(256)S(1)}, u32[]{:S(2)}) copy-start(f32[256]{0:T(256)S(1)} %get-tuple-element.49) | copy-start | bytes 3076
  60.4 16.7 %copy-start.29 = (f32[2,128]{1,0:T(2,128)}, f32[2,128]{1,0:T(2,128)S(1)}, u32[]{:S(2)}) copy-start(f32[2,128]{1,0:T(2,128)S(1)} %multiply_reduce_fusion.6) | copy-start | bytes 3076
  60.5 16.7 %copy-start.26 = (f32[256]{0:T(256)}, f32[256]{0:T(256)S(1)}, u32[]{:S(2)}) copy-start(f32[256]{0:T(256)S(1)} %bitcast_rsqrt_fusion) | copy-start | bytes 3076
  61.7 12.3 %copy-start.17 = (bf16[256,768]{1,0:T(8,128)(2,1)}, bf16[256,768]{1,0:T(8,128)(2,1)S(1)}, u32[]{:S(2)}) copy-start(bf16[256,768]{1,0:T(8,128)(2,1)S(1)} %add_convert_fusion.1) | copy-start | bytes 1179652
  77.1 62.4 %copy-start.3 = (bf16[2,128,768]{2,1,0:T(8,128)(2,1)S(1)}, bf16[2,128,768]{2,1,0:T(8,128)(2,1)}, u32[]{:S(2)}) copy-start(bf16[2,128,768]{2,1,0:T(8,128)(2,1)} %param.27) | copy-start | bytes 1179652
  78.1 217.2 %all-gather.10.cloned.1.call-start = ((), (), s32[]{:S(2)}) async-start(), calls=%async_computation.7 | async-start | bytes 1216512 | tf_op jit(solution)/shard_map/all_gather | solution.py:116
  78.7 282.2 %all-gather.12.cloned.1.call-start = ((), (), s32[]{:S(2)}) async-start(), calls=%async_computation.8 | async-start | bytes 4866048 | tf_op jit(solution)/shard_map/all_gather | solution.py:120
  79.3 458.0 %reduce-scatter.6.cloned.1.call-start = ((), (), s32[]{:S(2)}) async-start(), calls=%async_computation.10 | async-start | bytes 7077888 | tf_op jit(solution)/shard_map/reduce_scatter | solution.py:251
  81.6 172.3 %copy-start.11 = (bf16[2,128,12,64]{1,0,3,2:T(2,128)(2,1)}, bf16[2,128,12,64]{1,0,3,2:T(2,128)(2,1)S(1)}, u32[]{:S(2)}) copy-start(bf16[2,128,12,64]{1,0,3,2:T(2,128)(2,1)S(1)} %reshape_reshape.10) | copy-start | bytes 1179652
  253.9 3.3 copy-start.16
  257.2 5.3 copy-start
  257.2 5.3 copy-start.22
  257.3 5.3 copy-start.15
  262.5 7.4 copy-start.20
  262.6 32.8 %copy-start.2 = (bf16[2,128,768]{2,1,0:T(8,128)(2,1)S(1)}, bf16[2,128,768]{2,1,0:T(8,128)(2,1)}, u32[]{:S(2)}) copy-start(bf16[2,128,768]{2,1,0:T(8,128)(2,1)} %param.14) | copy-start | bytes 1179652
  295.3 4.3 copy-start.21
  295.4 4.3 copy-start.23
  297.4 0.9 copy-start.8
  298.5 0.6 copy-start.31
  360.8 9.5 copy-start.9
  360.8 9.5 copy-start.28
  360.8 9.5 copy-start.35
  370.4 2.3 copy-start.18
  370.4 2.2 copy-start.32
  370.4 2.6 copy-start.4
  372.6 2.1 copy-start.19
  373.0 0.9 copy-start.6
  373.0 0.9 copy-start.33
  373.9 0.8 copy-start.13
  397.4 8.6 copy-start.12
  405.9 3.7 copy-start.1
  420.3 221.2 %reduce-scatter.10.cloned.1.call-start = ((), (), s32[]{:S(2)}) async-start(), calls=%async_computation.12 | async-start | bytes 2433024 | tf_op jit(solution)/shard_map/reduce_scatter | solution.py:273
  423.4 360.1 %reduce-scatter.12.cloned.1.call-start = ((), (), s32[]{:S(2)}) async-start(), calls=%async_computation.13 | async-start | bytes 9732096 | tf_op jit(solution)/shard_map/reduce_scatter | solution.py:277
  430.4 494.5 %reduce-scatter.14.cloned.1.call-start = ((), (), s32[]{:S(2)}) async-start(), calls=%async_computation.14 | async-start | bytes 9732096 | tf_op jit(solution)/shard_map/reduce_scatter | solution.py:279
  438.2 611.7 %reduce-scatter.8.cloned.1.call-start = ((), (), s32[]{:S(2)}) async-start(), calls=%async_computation.11 | async-start | bytes 7299072 | tf_op jit(solution)/shard_map/reduce_scatter | solution.py:271
  542.6 0.7 copy-start.34
  542.6 1.0 copy-start.5
  542.6 1.7 copy-start.10
  544.2 6.1 copy-start.14
  544.2 6.4 copy-start.25
  544.2 6.4 copy-start.36
  550.6 1.8 copy-start.30
  550.6 1.8 copy-start.27
  550.6 47.6 %copy-start.7 = (f32[256,768]{1,0:T(8,128)S(1)}, f32[256,768]{1,0:T(8,128)}, u32[]{:S(2)}) copy-start(f32[256,768]{1,0:T(8,128)} %copy-done.6) | copy-start | bytes 2359300
Sparse Core Ops, SparseCore 0:
  11.0 62.9 all-gather.5
  77.0 62.4 all-gather.13
  142.3 97.8 all-gather.7
  243.0 52.3 all-gather.9
  298.2 62.6 all-gather.11
  420.5 116.7 reduce-scatter.5
  543.1 98.3 reduce-scatter.9
  649.0 134.5 reduce-scatter.11
  790.0 134.7 reduce-scatter.13
  931.9 118.0 reduce-scatter.7
where the time goes:
time: 1060 us
  waiting for transfers between devices  795 us (75%)
  matrix products  91.1 us (9%)
  blocking collectives  83.2 us (8%)
  local copies, waits for them, and re-layouts  46.4 us (4%)
  other arithmetic  24.6 us (2%)
  between operations  14.9 us (1%)
    reduce_scatter x1, waiting for transfers between devices, body(): lax.psum_scatter(grad_fc_weight, ('dp', 'ctx'), scatter_dimension=0, tile...  142 us
    reduce_scatter x1, waiting for transfers between devices, body(): lax.psum_scatter(grad_out_weight, ('dp', 'ctx'), scatter_dimension=0, til...  141 us
    reduce_scatter x1, waiting for transfers between devices, body(): lax.psum_scatter(grad_qkv_weight, ('dp', 'ctx'), scatter_dimension=0, til...  125 us
    all_gather x1, waiting for transfers between devices, body(): remote = lax.all_gather(key_value, 'ctx', axis=1, tiled=True)  95.2 us
    reduce_scatter x1, waiting for transfers between devices, body(): lax.psum_scatter(grad_kv_all.astype(jnp.bfloat16), 'ctx', scatter_dimensi...  93 us
    unnamed x2, blocking collectives  83.2 us
    all_gather x1, waiting for transfers between devices, body(): lax.all_gather(w_fc, ('dp', 'ctx'), axis=0, tiled=True)  60.5 us
    all_gather x1, waiting for transfers between devices, body(): lax.all_gather(w_out, ('dp', 'ctx'), axis=0, tiled=True)  57.9 us
  transfers between devices with their start and end apart: 10, of which 10 were waited for; matrix products, arithmetic and copies ran while one was open for 9% of the time, Pallas kernels for 0%

commit v1 on v0

--- a/solution.py
+++ b/solution.py
@@ -1,8 +1,11 @@
+import functools
 import math
 
 import jax
 import jax.numpy as jnp
 from jax import lax
+from jax.experimental import pallas as pl
+from jax.experimental.pallas import tpu as pltpu
 from jax.sharding import PartitionSpec as P
 
 H = 12
@@ -92,7 +95,7 @@
     return (grad_query, grad_keys, grad_values)
 
 
-def body(
+def plain_body(
     tokens,
     ln1_gain,
     ln1_bias,
@@ -282,6 +285,371 @@
     return (result, grad_input) + tuple(gradients)
 
 
+def axis_bits(axis):
+    size = lax.axis_size(axis)
+    return [(axis, 1 << k) for k in reversed(range(size.bit_length() - 1))]
+
+
+def swap(values, bit):
+    axis, mask = bit
+    return lax.ppermute(values, axis, [(i, i ^ mask) for i in range(lax.axis_size(axis))])
+
+
+def bit_value(bit):
+    axis, mask = bit
+    return (lax.axis_index(axis) // mask) % 2
+
+
+def in_order(mine, other, bit, dim):
+    upper = bit_value(bit) == 1
+    return jnp.stack([jnp.where(upper, other, mine), jnp.where(upper, mine, other)], axis=dim)
+
+
+def gather_bit(values, bit, dim):
+    return in_order(values, swap(values, bit), bit, dim)
+
+
+def take(values, index, dim):
+    return lax.dynamic_index_in_dim(values, index, dim, keepdims=False)
+
+
+def scatter_bit(values, bit, dim):
+    here = bit_value(bit)
+    sent = swap(take(values, 1 - here, dim), bit)
+    kept = take(values, here, dim).astype(jnp.float32)
+    return (kept + sent.astype(jnp.float32)).astype(values.dtype)
+
+
+def trade_bit(values, bit, dim):
+    here = bit_value(bit)
+    return in_order(take(values, here, dim), swap(take(values, 1 - here, dim), bit), bit, dim)
+
+
+def gather_rows(shard, order, bits):
+    held = []
+    values = shard
+    for bit in order:
+        held = sorted(held + [bit], key=bits.index)
+        values = gather_bit(values, bit, held.index(bit))
+    return values.reshape((-1,) + shard.shape[1:])
+
+
+def scatter_rows(values, order, bits):
+    count = 1 << len(bits)
+    values = values.reshape((2,) * len(bits) + (values.shape[0] // count,) + values.shape[1:])
+    left = list(bits)
+    for bit in order:
+        values = scatter_bit(values, bit, left.index(bit))
+        left.remove(bit)
+    return values
+
+
+def turned(items, steps):
+    steps = steps % max(len(items), 1)
+    return items[steps:] + items[:steps]
+
+
+def dot_last(left, right):
+    return lax.dot_general(left, right, (((1,), (1,)), ((), ())), preferred_element_type=jnp.float32)
+
+
+def dot_first(left, right):
+    return lax.dot_general(left, right, (((0,), (0,)), ((), ())), preferred_element_type=jnp.float32)
+
+
+def seen_scores(keys, queries, start):
+    scores = dot_last(keys, queries)
+    key_pos = lax.broadcasted_iota(jnp.int32, scores.shape, 0)
+    query_pos = lax.broadcasted_iota(jnp.int32, scores.shape, 1) + start
+    return jnp.where(key_pos <= query_pos, scores, NEG)
+
+
+def attend_kernel(heads, block, qkv_ref, out_ref):
+    wide = heads * HD
+    for head in range(heads):
+        at = head * HD
+        for low in range(0, qkv_ref.shape[0], block):
+            high = low + block
+            queries = qkv_ref[low:high, at : at + HD] * (1.0 / math.sqrt(HD))
+            keys = qkv_ref[:high, wide + at : wide + at + HD]
+            values = qkv_ref[:high, 2 * wide + at : 2 * wide + at + HD]
+            scores = seen_scores(keys, queries, low)
+            weights = jnp.exp(scores - jnp.max(scores, axis=0, keepdims=True))
+            total = jnp.sum(weights, axis=0, keepdims=True)
+            mixed = dot_first(values, weights.astype(jnp.bfloat16)) / total
+            out_ref[low:high, at : at + HD] = mixed.T.astype(jnp.bfloat16)
+
+
+def attend_grad_kernel(heads, block, qkv_ref, grad_ref, out_ref, keys_acc, values_acc):
+    wide = heads * HD
+    factor = 1.0 / math.sqrt(HD)
+    for head in range(heads):
+        at = head * HD
+        keys_acc[...] = jnp.zeros_like(keys_acc)
+        values_acc[...] = jnp.zeros_like(values_acc)
+        for low in range(0, qkv_ref.shape[0], block):
+            high = low + block
+            queries = qkv_ref[low:high, at : at + HD] * factor
+            keys = qkv_ref[:high, wide + at : wide + at + HD]
+            values = qkv_ref[:high, 2 * wide + at : 2 * wide + at + HD]
+            grads = grad_ref[low:high, at : at + HD]
+            scores = seen_scores(keys, queries, low)
+            weights = jnp.exp(scores - jnp.max(scores, axis=0, keepdims=True))
+            probs = weights / jnp.sum(weights, axis=0, keepdims=True)
+            grad_probs = dot_last(values, grads)
+            delta = jnp.sum(probs * grad_probs, axis=0, keepdims=True)
+            grad_scores = (probs * (grad_probs - delta)).astype(jnp.bfloat16)
+            values_acc[:high] += jnp.dot(
+                probs.astype(jnp.bfloat16), grads, preferred_element_type=jnp.float32
+            )
+            keys_acc[:high] += jnp.dot(grad_scores, queries, preferred_element_type=jnp.float32)
+            grad_queries = dot_first(keys, grad_scores) * factor
+            out_ref[low:high, at : at + HD] = grad_queries.T.astype(jnp.bfloat16)
+        out_ref[:, wide + at : wide + at + HD] = keys_acc[...].astype(jnp.bfloat16)
+        out_ref[:, 2 * wide + at : 2 * wide + at + HD] = values_acc[...].astype(jnp.bfloat16)
+
+
+VMEM_LIMIT = 48 * 1024 * 1024
+
+
+def attend(qkv, heads):
+    rows = qkv.shape[0]
+    return pl.pallas_call(
+        functools.partial(attend_kernel, heads, min(rows, 256)),
+        out_shape=jax.ShapeDtypeStruct((rows, heads * HD), jnp.bfloat16),
+        compiler_params=pltpu.CompilerParams(vmem_limit_bytes=VMEM_LIMIT),
+        name="attend",
+    )(qkv)
+
+
+def attend_back(qkv, grads, heads):
+    rows = qkv.shape[0]
+    return pl.pallas_call(
+        functools.partial(attend_grad_kernel, heads, min(rows, 256)),
+        out_shape=jax.ShapeDtypeStruct(qkv.shape, jnp.bfloat16),
+        scratch_shapes=[pltpu.VMEM((rows, HD), jnp.float32), pltpu.VMEM((rows, HD), jnp.float32)],
+        compiler_params=pltpu.CompilerParams(vmem_limit_bytes=VMEM_LIMIT),
+        name="attend_back",
+    )(qkv, grads)
+
+
+def normalize(values):
+    average = jnp.mean(values, axis=-1, keepdims=True)
+    centered = values - average
+    variance = jnp.mean(centered * centered, axis=-1, keepdims=True)
+    scale = lax.rsqrt(variance + EPS)
+    return centered * scale, scale
+
+
+def normalize_back(grad_normed, gain, unit, scale):
+    inner = grad_normed * gain
+    return scale * (
+        inner
+        - jnp.mean(inner, axis=-1, keepdims=True)
+        - unit * jnp.mean(inner * unit, axis=-1, keepdims=True)
+    )
+
+
+def split_body(
+    tokens,
+    ln1_gain,
+    ln1_bias,
+    w_qkv,
+    b_qv,
+    w_proj,
+    b_proj,
+    ln2_gain,
+    ln2_bias,
+    w_fc,
+    b_fc,
+    w_out,
+    b_out,
+    cotangent,
+):
+    f32, bf16 = jnp.float32, jnp.bfloat16
+    count_seq, group_len, model_width = tokens.shape
+    rows_total = count_seq * group_len
+    dp_bits, ctx_bits = axis_bits("dp"), axis_bits("ctx")
+    bits = dp_bits + ctx_bits
+    seq_bit, team_bits = ctx_bits[0], ctx_bits[1:]
+    ctx_size = lax.axis_size("ctx")
+    devices = ctx_size * lax.axis_size("dp")
+    team = 1 << len(team_bits)
+    heads = H // team
+    wide = heads * HD
+    sequence = bit_value(seq_bit)
+    member = lax.axis_index("ctx") % team
+    near, far = dp_bits[-1], seq_bit
+    middle = [bit for bit in turned(team_bits, 1) + dp_bits[:-1]]
+
+    def gather_order(turn):
+        return [far] + turned(middle, turn) + [near]
+
+    def scatter_order(turn):
+        return [near] + turned(middle, turn) + [far]
+
+    mine = take(tokens, sequence, 0)
+    theirs = swap(take(tokens, 1 - sequence, 0), seq_bit)
+    pair = in_order(mine, theirs, seq_bit, 0)
+    half = model_width // 2
+    sides = []
+    for side, order in ((0, team_bits), (1, team_bits[::-1])):
+        held = []
+        part = pair[..., side * half : (side + 1) * half]
+        for bit in order:
+            held = sorted(held + [bit], key=team_bits.index)
+            part = gather_bit(part, bit, 1 + held.index(bit))
+        sides.append(part.reshape(ctx_size * group_len, half))
+    long_tokens = jnp.concatenate(sides, axis=1)
+
+    vectors = (ln1_gain, ln1_bias, b_qv, b_proj, ln2_gain, ln2_bias, b_fc, b_out)
+    sizes = [vector.shape[0] for vector in vectors]
+    starts = [sum(sizes[:k]) for k in range(len(sizes))]
+    packed = jnp.concatenate(vectors)[None, :]
+    all_vectors = gather_rows(packed, bits[::-1], bits).astype(f32)
+    (gain_one, bias_one, qv_bias, proj_bias, gain_two, bias_two, fc_bias, out_bias) = (
+        all_vectors[:, start : start + size].reshape(devices * size)
+        for start, size in zip(starts, sizes)
+    )
+    rows_own = w_qkv.shape[0]
+    columns = w_qkv.reshape(rows_own, 3, team, wide).transpose(2, 0, 1, 3)
+    columns = columns.reshape((2,) * len(team_bits) + (rows_own, 3 * wide))
+    for k in reversed(range(len(team_bits))):
+        columns = trade_bit(columns, team_bits[k], k)
+    for bit in [seq_bit] + dp_bits[::-1]:
+        columns = gather_bit(columns, bit, 0)
+    qkv_weight = columns.reshape(devices * rows_own, 3 * wide)
+
+    proj_weight = gather_rows(w_proj, gather_order(0), bits)
+    fc_weight = gather_rows(w_fc, gather_order(1), bits)
+    out_weight = gather_rows(w_out, gather_order(2), bits)
+
+    unit_long, _ = normalize(long_tokens.astype(f32))
+    normed_long = (unit_long * gain_one + bias_one).astype(bf16)
+    team_bias = take(qv_bias.reshape(2, team, wide), member, 1)
+    bias_row = jnp.concatenate([team_bias[0], jnp.zeros((wide,), f32), team_bias[1]])
+    qkv = (jnp.dot(normed_long, qkv_weight, preferred_element_type=f32) + bias_row).astype(bf16)
+    attended = attend(qkv, heads)
+
+    def to_rows(values):
+        parts = lax.all_to_all(
+            values.reshape(ctx_size, group_len, wide), "ctx", 0, 0, tiled=True
+        )
+        parts = parts.reshape(count_seq, team, group_len, wide).transpose(0, 2, 1, 3)
+        return parts.reshape(rows_total, model_width)
+
+    def to_heads(values):
+        parts = values.reshape(count_seq, group_len, team, wide).transpose(0, 2, 1, 3)
+        parts = parts.reshape(ctx_size, group_len, wide)
+        return lax.all_to_all(parts, "ctx", 0, 0, tiled=True).reshape(ctx_size * group_len, wide)
+
+    merged = to_rows(attended)
+
+    inputs = tokens.astype(f32).reshape(rows_total, model_width)
+    middle_rows = inputs + jnp.dot(merged, proj_weight, preferred_element_type=f32) + proj_bias
+    unit_two, scale_two = normalize(middle_rows)
+    normed_two = (unit_two * gain_two + bias_two).astype(bf16)
+    pre_act = jnp.dot(normed_two, fc_weight, preferred_element_type=f32) + fc_bias
+    activated32, gelu_pull = jax.vjp(gelu_tanh, pre_act)
+    activated = activated32.astype(bf16)
+    result = middle_rows + jnp.dot(activated, out_weight, preferred_element_type=f32) + out_bias
+    result = result.astype(bf16).reshape(tokens.shape)
+
+    grad_top = cotangent.reshape(rows_total, model_width)
+    grad_top32 = grad_top.astype(f32)
+    grad_out_bias = jnp.sum(grad_top32, axis=0)
+    grad_out_weight = scatter_rows(outer_sum(activated, grad_top).astype(bf16), scatter_order(0), bits)
+    grad_pre = gelu_pull(back_through(grad_top, out_weight))[0].astype(bf16)
+    grad_fc_bias = jnp.sum(grad_pre.astype(f32), axis=0)
+    grad_fc_weight = scatter_rows(outer_sum(normed_two, grad_pre).astype(bf16), scatter_order(1), bits)
+    grad_normed_two = back_through(grad_pre, fc_weight)
+    grad_gain_two = jnp.sum(grad_normed_two * unit_two, axis=0)
+    grad_bias_two = jnp.sum(grad_normed_two, axis=0)
+    grad_middle = grad_top32 + normalize_back(grad_normed_two, gain_two, unit_two, scale_two)
+    grad_branch = grad_middle.astype(bf16)
+    grad_proj_bias = jnp.sum(grad_branch.astype(f32), axis=0)
+    grad_proj_weight = scatter_rows(outer_sum(merged, grad_branch).astype(bf16), scatter_order(2), bits)
+    grad_heads = to_heads(back_through(grad_branch, proj_weight).astype(bf16))
+    grad_qkv = attend_back(qkv, grad_heads, heads)
+
+    grad_long = back_through(grad_qkv, qkv_weight)
+    grad_gain_one = jnp.sum(grad_long * unit_long, axis=0)
+    grad_bias_one = jnp.sum(grad_long, axis=0)
+    blocks = grad_long.astype(bf16).reshape(
+        (2,) * len(ctx_bits) + (group_len, model_width)
+    )
+    sides = []
+    for side, order in ((0, team_bits), (1, team_bits[::-1])):
+        left = list(team_bits)
+        part = blocks[..., side * half : (side + 1) * half]
+        for bit in order:
+            part = scatter_bit(part, bit, 1 + left.index(bit))
+            left.remove(bit)
+        sides.append(part)
+    part = jnp.concatenate(sides, axis=-1)
+    grad_normed_one = trade_bit(part, seq_bit, 0).astype(f32)
+    unit_one, scale_one = normalize(tokens.astype(f32))
+    grad_input = grad_middle.reshape(tokens.shape) + normalize_back(
+        grad_normed_one, gain_one, unit_one, scale_one
+    )
+
+    parts = outer_sum(normed_long, grad_qkv).astype(bf16)
+    parts = parts.reshape((2,) * len(bits) + (rows_own, 3 * wide))
+    left = list(bits)
+    for bit in dp_bits[::-1] + [seq_bit]:
+        parts = scatter_bit(parts, bit, left.index(bit))
+        left.remove(bit)
+    for k in range(len(team_bits)):
+        parts = trade_bit(parts, team_bits[k], k)
+    grad_qkv_weight = (
+        parts.reshape(team, rows_own, 3, wide).transpose(1, 2, 0, 3).reshape(w_qkv.shape).astype(f32)
+    )
+
+    sums = jnp.sum(grad_qkv.astype(f32), axis=0).reshape(3, 1, wide)
+    placed = lax.dynamic_update_index_in_dim(
+        jnp.zeros((2, team, wide), f32), jnp.concatenate([sums[:1], sums[2:]]), member, 1
+    )
+    totals = (
+        grad_gain_one,
+        grad_bias_one,
+        placed.reshape(2 * model_width),
+        grad_proj_bias,
+        grad_gain_two,
+        grad_bias_two,
+        grad_fc_bias,
+        grad_out_bias,
+    )
+    spread = jnp.concatenate([total.reshape(devices, -1) for total in totals], axis=1)
+    own = scatter_rows(spread, scatter_order(0), bits)[0]
+    (g_gain_one, g_bias_one, g_qv, g_proj, g_gain_two, g_bias_two, g_fc, g_out) = (
+        own[start : start + size] for start, size in zip(starts, sizes)
+    )
+    return (
+        result,
+        grad_input,
+        g_gain_one,
+        g_bias_one,
+        grad_qkv_weight,
+        g_qv,
+        grad_proj_weight.astype(f32),
+        g_proj,
+        g_gain_two,
+        g_bias_two,
+        grad_fc_weight.astype(f32),
+        g_fc,
+        grad_out_weight.astype(f32),
+        g_out,
+    )
+
+
+def body(tokens, *others):
+    ctx_size, dp_size = lax.axis_size("ctx"), lax.axis_size("dp")
+    powers = ctx_size & (ctx_size - 1) == 0 and dp_size & (dp_size - 1) == 0
+    if powers and dp_size > 1 and ctx_size > 2 and tokens.shape[0] == 2 and H % (ctx_size // 2) == 0:
+        return split_body(tokens, *others)
+    return plain_body(tokens, *others)
+
+
 def solution(mesh):
     placed = (
         P("dp", "ctx", None),

time: 1060 us -> 357 us (0.34)
  waiting for transfers between devices: 795 us -> 147 us
  blocking collectives: 83.2 us -> 0 us
  starting transfers between devices: 1.18 us -> 73 us
  matrix products: 91.1 us -> 31.1 us
  Pallas kernels: 0 us -> 15.1 us
  between operations: 14.9 us -> 2.87 us
  other arithmetic: 24.6 us -> 35.2 us
    reduce_scatter x5 -> x0, waiting for transfers between devices: 543 us -> none  [the longest x1 142 us: body(): lax.psum_scatter(grad_fc_weight, ('dp', 'ctx'), scatter_dimension=0, tile...]
    all_gather x5 -> x0, waiting for transfers between devices: 250 us -> none  [the longest x1 95.2 us: body(): remote = lax.all_gather(key_value, 'ctx', axis=1, tiled=True)]
    ppermute x0 -> x60, waiting for transfers between devices: none -> 139 us  [swap(): lax.ppermute(values, axis, [(i, i ^ mask) for i in range(lax.axis_size(ax...]
    unnamed x2 -> x0, blocking collectives: 83.2 us -> none
    ppermute x0 -> x60, starting transfers between devices: none -> 64.1 us  [swap(): lax.ppermute(values, axis, [(i, i ^ mask) for i in range(lax.axis_size(ax...]
    dot_general x10 -> x4, matrix products: 57.6 us -> 8.74 us  [the longest x1 2.71 us: split_body(): jnp.dot(activated, out_weight, preferred_element_type=f32)]
    pallas_call x0 -> x2, Pallas kernels: none -> 15.1 us  [the longest x1 9.89 us: attend_back(): pl.pallas_call(functools.partial(attend_grad_kernel, heads, min(rows, 256...]
    another operation x1 -> x61, other arithmetic: 0.01 us -> 14.6 us  [in_order(): jnp.stack([jnp.where(upper, other, mine), jnp.where(upper, mine, other)],...]
  transfers between devices with their start and end apart: 10 -> 62, of which waited for: 10 -> 33; matrix products, arithmetic and copies ran while one was open for 9% -> 22% of each run, Pallas kernels for 0% -> 4%
where the time goes in v1:
time: 357 us; the launch traced here: 350 us
  waiting for transfers between devices  147 us (41%)
  starting transfers between devices  73 us (20%)
  local copies, waits for them, and re-layouts  46.1 us (13%)
  other arithmetic  35.2 us (10%)
  matrix products  31.1 us (9%)
  Pallas kernels  15.1 us (4%)
    ppermute x60, waiting for transfers between devices, swap(): lax.ppermute(values, axis, [(i, i ^ mask) for i in range(lax.axis_size(ax...  139 us
    ppermute x60, starting transfers between devices, swap(): lax.ppermute(values, axis, [(i, i ^ mask) for i in range(lax.axis_size(ax...  64.1 us
    another operation x61, other arithmetic, in_order(): jnp.stack([jnp.where(upper, other, mine), jnp.where(upper, mine, other)],...  14.6 us
    dynamic_slice x7, local copies, waits for them, and re-layouts, take(): return lax.dynamic_index_in_dim(values, index, dim, keepdims=False)  14.4 us
    dot_general x4, matrix products, outer_sum(): lax.dot_general(left, right, (((0,), (0,)), ((), ())), preferred_element_...  12.4 us
    convert_element_type x19, other arithmetic, scatter_bit(): return (kept + sent.astype(jnp.float32)).astype(values.dtype)  11.2 us
    dot_general x4, matrix products, back_through(): lax.dot_general(grad_rows, weight_mat, (((1,), (1,)), ((), ())), preferre...  9.9 us
    pallas_call x1, Pallas kernels, attend_back(): pl.pallas_call(functools.partial(attend_grad_kernel, heads, min(rows, 256...  9.89 us
  transfers between devices with their start and end apart: 62, of which 33 were waited for; matrix products, arithmetic and copies ran while one was open for 22% of the time, Pallas kernels for 4%

profile of v1, /device:TPU:0, one launch (start us, length us, event | category | flops | bytes accessed | tf_op | source)
XLA Modules:
  0.0 350.3 jit_solution(2848168507692591103)
XLA Ops:
  0.7 5.5 %concatenate.36 = bf16[288]{0:T(512)(128)(2,1)S(1)} concatenate(bf16[24]{0:T(256)(128)(2,1)} %param.15, bf16[24]{0:T(256)(128)(2,1)} %param.16, bf16[48]{0:T(256)(128)(2,1)} %param.18, bf16[24]{0:T(256)(128)(2,1)} %param.20, bf16[24]{0:T(256)(128)(2,1)} %param.21, bf16[24]{0:T(256)(128)(2,1)} %param.22, bf16[96]{0:T(256)(128)(2,1)} %param.24, bf16[24]{0:T(256)(128)(2,1)} %param.26), dimensions={0} | concatenate | bytes 1152 | tf_op jit(solution)/shard_map/concatenate | solution.py:508
  6.2 3.0 collective-permute-start.5
  9.2 2.6 collective-permute-start.15
  16.7 2.6 collective-permute-start.25
  20.9 12.5 %collective-permute-done.7 = bf16[2,2,1,288]{3,1,0,2:T(2,128)(2,1)S(1)} collective-permute-done((bf16[2,2,1,288]{3,1,0,2:T(2,128)(2,1)S(1)}, bf16[2,2,1,288]{3,1,0,2:T(2,128)(2,1)S(1)}, u32[]{:S(2)}, u32[]{:S(2)}) %collective-permute-start.7) | collective-permute-done | bytes 2336 | tf_op jit(solution)/shard_map/ppermute | solution.py:295
  46.5 2.3 collective-permute-start.12
  54.8 2.5 collective-permute-done.3
  57.8 5.7 %collective-permute-done.1 = bf16[2,128,384]{2,1,0:T(8,128)(2,1)S(1)} collective-permute-done((bf16[2,128,384]{2,1,0:T(8,128)(2,1)S(1)}, bf16[2,128,384]{2,1,0:T(8,128)(2,1)S(1)}, u32[]{:S(2)}, u32[]{:S(2)}) %collective-permute-start.1) | collective-permute-done | bytes 196640 | tf_op jit(solution)/shard_map/ppermute | solution.py:295
  69.4 3.6 %collective-permute-done.4 = bf16[2,2,128,384]{3,2,0,1:T(8,128)(2,1)S(1)} collective-permute-done((bf16[2,2,128,384]{3,2,0,1:T(8,128)(2,1)S(1)}, bf16[2,2,128,384]{3,2,0,1:T(8,128)(2,1)S(1)}, u32[]{:S(2)}, u32[]{:S(2)}) %collective-permute-start.4) | collective-permute-done | bytes 393248 | tf_op jit(solution)/shard_map/ppermute | solution.py:295
  73.3 2.4 collective-permute-done.2
  76.3 9.5 %collective-permute-done.27 = bf16[2,2,96,768]{3,2,1,0:T(8,128)(2,1)S(1)} collective-permute-done((bf16[2,2,96,768]{3,2,1,0:T(8,128)(2,1)S(1)}, bf16[2,2,96,768]{3,2,1,0:T(8,128)(2,1)S(1)}, u32[]{:S(2)}, u32[]{:S(2)}) %collective-permute-start.27) | collective-permute-done | bytes 589856 | tf_op jit(solution)/shard_map/ppermute | solution.py:295
  88.4 2.3 collective-permute-start.23
  91.7 19.8 %collective-permute-done.28 = bf16[2,2,2,96,768]{4,3,2,1,0:T(8,128)(2,1)S(1)} collective-permute-done((bf16[2,2,2,96,768]{4,3,2,1,0:T(8,128)(2,1)S(1)}, bf16[2,2,2,96,768]{4,3,2,1,0:T(8,128)(2,1)S(1)}, u32[]{:S(2)}, u32[]{:S(2)}) %collective-permute-start.28) | collective-permute-done | bytes 1179680 | tf_op jit(solution)/shard_map/ppermute | solution.py:295
  117.1 2.7 add_convert_fusion.qkv_ref
  119.8 5.2 %attend.1 = bf16[1024,192]{1,0:T(8,128)(2,1)S(1)} custom-call(bf16[1024,576]{1,0:T(8,128)(2,1)S(1)} %add_convert_fusion.qkv_ref), custom_call_target="tpu_custom_call" | custom-call | tf_op jit(solution)/shard_map/attend/pallas_call | solution.py:417
  126.0 4.6 %all-to-all-start = ((bf16[8,128,192]{1,2,0:T(8,128)(2,1)}), bf16[8,128,192]{1,2,0:T(8,128)(2,1)S(1)}, u32[]{:S(2)}, u32[]{:S(2)}) async-start(bf16[8,128,192]{1,2,0:T(8,128)(2,1)} %copy.83), calls=%async_computation | async-start | bytes 786432 | tf_op jit(solution)/shard_map/all_to_all | solution.py:535
  135.3 7.6 %all-to-all-done = bf16[8,128,192]{1,2,0:T(8,128)(2,1)S(1)} async-done(((bf16[8,128,192]{1,2,0:T(8,128)(2,1)}), bf16[8,128,192]{1,2,0:T(8,128)(2,1)S(1)}, u32[]{:S(2)}, u32[]{:S(2)}) %all-to-all-start) | async-done | bytes 393248 | tf_op jit(solution)/shard_map/all_to_all | solution.py:535
  145.5 2.0 select_bitcast_fusion.1
  149.1 2.0 select_bitcast_fusion.3
  153.1 3.3 convert_reduce_fusion.1
  160.3 3.8 %convolution_convert_fusion.1 = bf16[768,3072]{1,0:T(8,128)(2,1)} fusion(bf16[256,3072]{1,0:T(8,128)(2,1)S(1)} %get-tuple-element.124, f32[256,768]{1,0:T(8,128)S(1)} %get-tuple-element.120, f32[768]{0:T(1024)S(1)} %add.428, f32[768]{0:T(1024)S(1)} %mul.160, f32[256]{0:T(256)S(1)} %add_rsqrt_fusion.2, f32[256]{0:T(256)S(1)} %broadcast_multiply_fusion.6), kind=kOutput, calls=%fused_computation.1 | convolution fusion | flops 1211301888 | bytes 7086080 | tf_op jit(solution)/shard_map/dot_general | solution.py:31
  164.1 4.5 %convolution_convert_fusion = bf16[3072,768]{1,0:T(8,128)(2,1)} fusion(bf16[256,768]{1,0:T(8,128)(2,1)S(1)} %bitcast.476, f32[256,3072]{1,0:T(8,128)S(1)} %convolution_add_fusion), kind=kOutput, calls=%fused_computation | convolution fusion | flops 1217396736 | bytes 8257536 | tf_op jit(solution)/shard_map/dot_general | solution.py:31
  168.6 2.7 fusion.21
  174.1 4.3 %all-to-all-start.1 = ((bf16[8,128,192]{1,2,0:T(8,128)(2,1)}), bf16[8,128,192]{1,2,0:T(8,128)(2,1)}, u32[]{:S(2)}, u32[]{:S(2)}) async-start(bf16[8,128,192]{1,2,0:T(8,128)(2,1)} %bitcast.96), calls=%async_computation.1 | async-start | bytes 786432 | tf_op jit(solution)/shard_map/all_to_all | solution.py:544
  178.7 5.1 %constant_dynamic-slice_fusion.4 = (bf16[2,1,2,2,2,24,3072]{6,5,4,3,2,1,0:T(8,128)(2,1)}, bf16[2,1,2,2,2,24,3072]{6,5,4,3,2,1,0:T(8,128)(2,1)}) fusion(bf16[2,2,2,2,2,24,3072]{6,5,4,3,2,1,0:T(8,128)(2,1)} %bitcast.446, s32[]{:T(128)S(6)} %select_n.829, s32[]{:T(128)S(6)} %select_n.830), kind=kLoop, calls=%fused_computation.256 | loop fusion | bytes 9437192 | tf_op jit(solution)/shard_map/jit(dynamic_index_in_dim)/dynamic_slice | solution.py:313
  186.6 3.3 copy.145
  190.4 4.2 %constant_dynamic-slice_fusion.2 = (bf16[2,1,2,2,2,96,768]{6,5,4,3,2,1,0:T(8,128)(2,1)}, bf16[2,1,2,2,2,96,768]{6,5,4,3,2,1,0:T(8,128)(2,1)S(1)}) fusion(bf16[2,2,2,2,2,96,768]{6,5,4,3,2,1,0:T(8,128)(2,1)} %bitcast.461, s32[]{:T(128)S(6)} %select_n.829, s32[]{:T(128)S(6)} %select_n.830), kind=kLoop, calls=%fused_computation.254 | loop fusion | bytes 9437192 | tf_op jit(solution)/shard_map/jit(dynamic_index_in_dim)/dynamic_slice | solution.py:313
  200.2 9.9 %attend_back.1 = bf16[1024,576]{1,0:T(8,128)(2,1)S(1)} custom-call(bf16[1024,576]{1,0:T(8,128)(2,1)S(1)} %add_convert_fusion.qkv_ref, bf16[1024,192]{1,0:T(8,128)(2,1)S(1)} %bitcast.445), custom_call_target="tpu_custom_call" | custom-call | tf_op jit(solution)/shard_map/attend_back/pallas_call | solution.py:427
  210.1 4.4 %fusion.93 = (f32[768]{0:T(1024)S(1)}, f32[768]{0:T(1024)S(1)}, bf16[1024,768]{1,0:T(8,128)(2,1)}) fusion(f32[1024]{0:T(1024)} %copy-done.41, f32[1024]{0:T(1024)} %copy-done.36, bf16[1024,384]{1,0:T(8,128)(2,1)} %bitcast.452, bf16[1024,384]{1,0:T(8,128)(2,1)} %bitcast.457, bf16[1024,576]{1,0:T(8,128)(2,1)S(1)} %attend_back.1, bf16[768,576]{1,0:T(8,128)(2,1)} %bitcast.478), kind=kOutput, calls=%fused_computation.326 | convolution fusion | flops 913832448 | bytes 5224448 | tf_op jit(solution)/shard_map/dot_general | solution.py:37
  215.9 3.7 %convolution_convert_fusion.3 = bf16[768,576]{0,1:T(8,128)(2,1)} fusion(bf16[1024,576]{1,0:T(8,128)(2,1)S(1)} %attend_back.1, f32[768]{0:T(1024)S(1)} %copy-done.40, f32[768]{0:T(1024)S(1)} %copy-done.31, f32[1024]{0:T(1024)S(1)} %copy-done.42, f32[1024]{0:T(1024)S(1)} %copy-done.37, bf16[1024,384]{1,0:T(8,128)(2,1)S(1)} %bitcast.453, ...), kind=kOutput, calls=%fused_computation.49 | convolution fusion | flops 913489920 | bytes 3651584 | tf_op jit(solution)/shard_map/dot_general | solution.py:31
  219.7 2.0 collective-permute-start.36
  229.8 2.6 collective-permute-done.38
  232.4 2.9 collective-permute-start.39
  241.9 6.0 %collective-permute-done.47 = bf16[2,2,24,768]{3,2,0,1:T(8,128)(2,1)S(1)} collective-permute-done((bf16[2,2,24,768]{3,2,0,1:T(8,128)(2,1)S(1)}, bf16[2,2,24,768]{3,2,0,1:T(8,128)(2,1)S(1)}, u32[]{:S(2)}, u32[]{:S(2)}) %collective-permute-start.47) | collective-permute-done | bytes 147488 | tf_op jit(solution)/shard_map/ppermute | solution.py:295
  248.0 2.5 collective-permute-start.48
  257.2 3.1 collective-permute-done.49
  262.0 4.7 %collective-permute-done.41 = bf16[2,2,2,24,576]{4,3,2,1,0:T(8,128)(2,1)S(1)} collective-permute-done((bf16[2,2,2,24,576]{4,3,2,1,0:T(8,128)(2,1)S(1)}, bf16[2,2,2,24,576]{4,3,2,1,0:T(8,128)(2,1)S(1)}, u32[]{:S(2)}, u32[]{:S(2)}) %collective-permute-start.41) | collective-permute-done | bytes 221216 | tf_op jit(solution)/shard_map/ppermute | solution.py:295
  266.8 3.1 collective-permute-start.42
  270.1 9.2 %collective-permute-done.42 = bf16[2,2,24,576]{3,2,1,0:T(8,128)(2,1)S(1)} collective-permute-done((bf16[2,2,24,576]{3,2,1,0:T(8,128)(2,1)S(1)}, bf16[2,2,24,576]{3,2,1,0:T(8,128)(2,1)S(1)}, u32[]{:S(2)}, u32[]{:S(2)}) %collective-permute-start.42) | collective-permute-done | bytes 110624 | tf_op jit(solution)/shard_map/ppermute | solution.py:295
  279.5 2.7 collective-permute-done.34
  282.6 2.6 fusion.1
  289.1 2.4 fusion
  293.1 18.8 %collective-permute-done.51 = bf16[2,2,2,24,3072]{4,3,1,2,0:T(8,128)(2,1)S(1)} collective-permute-done((bf16[2,2,2,24,3072]{4,3,1,2,0:T(8,128)(2,1)S(1)}, bf16[2,2,2,24,3072]{4,3,1,2,0:T(8,128)(2,1)S(1)}, u32[]{:S(2)}, u32[]{:S(2)}) %collective-permute-start.51) | collective-permute-done | bytes 1179680 | tf_op jit(solution)/shard_map/ppermute | solution.py:295
  316.6 2.7 collective-permute-done.56
  321.7 6.0 %collective-permute-done.52 = bf16[2,2,24,3072]{3,2,0,1:T(8,128)(2,1)} collective-permute-done((bf16[2,2,24,3072]{3,2,0,1:T(8,128)(2,1)}, bf16[2,2,24,3072]{3,2,0,1:T(8,128)(2,1)}, u32[]{:S(2)}, u32[]{:S(2)}) %collective-permute-start.52) | collective-permute-done | bytes 589856 | tf_op jit(solution)/shard_map/ppermute | solution.py:295
  330.6 3.1 collective-permute-done.57
  337.3 3.4 collective-permute-done.58
  342.1 5.4 %collective-permute-done.54 = bf16[24,3072]{1,0:T(8,128)(2,1)S(1)} collective-permute-done((bf16[24,3072]{1,0:T(8,128)(2,1)S(1)}, bf16[24,3072]{1,0:T(8,128)(2,1)S(1)}, u32[]{:S(2)}, u32[]{:S(2)}) %collective-permute-start.54) | collective-permute-done | bytes 147488 | tf_op jit(solution)/shard_map/ppermute | solution.py:295
  (372 shorter events, 116.5 us)
Async XLA Ops:
  6.2 7.5 %collective-permute-start.5 = (bf16[1,288]{1,0:T(2,128)(2,1)S(1)}, bf16[1,288]{1,0:T(2,128)(2,1)S(1)}, u32[]{:S(2)}, u32[]{:S(2)}) collective-permute-start(bf16[1,288]{1,0:T(2,128)(2,1)S(1)} %broadcast_in_dim.6), channel_id=1, source_target_pairs={{0,1},{1,0},{2,3},{3,2},{4,5},{5,4},{6,7},{7,6},{8,9},{9,8},{10,11... | collective-permute-start | bytes 1736 | tf_op jit(solution)/shard_map/ppermute | solution.py:295
  9.2 30.0 %collective-permute-start.15 = (bf16[24,768]{1,0:T(8,128)(2,1)}, bf16[24,768]{1,0:T(8,128)(2,1)S(1)}, u32[]{:S(2)}, u32[]{:S(2)}) collective-permute-start(bf16[24,768]{1,0:T(8,128)(2,1)} %param.19), channel_id=1, source_target_pairs={{0,4},{1,5},{2,6},{3,7},{4,0},{5,1},{6,2},{7,3},{8,12},{9,13},{10,... | collective-permute-start | bytes 110600 | tf_op jit(solution)/shard_map/ppermute | solution.py:295
  13.1 27.6 %collective-permute-start.10 = (bf16[2,24,576]{2,1,0:T(8,128)(2,1)S(1)}, bf16[2,24,576]{2,1,0:T(8,128)(2,1)S(1)}, u32[]{:S(2)}, u32[]{:S(2)}) collective-permute-start(bf16[2,24,576]{2,1,0:T(8,128)(2,1)S(1)} %dynamic-slice_bitcast_fusion.19), channel_id=1, source_target_pairs={{0,1},{1,0},{2,3},{3,2},{4,5},{5,4},{6,7},{7,6},{8,9},{9,8},{10,11... | collective-permute-start | bytes 165896 | tf_op jit(solution)/shard_map/ppermute | solution.py:295
  16.3 35.1 %collective-permute-start = (bf16[128,768]{1,0:T(8,128)(2,1)S(1)}, bf16[128,768]{1,0:T(8,128)(2,1)S(1)}, u32[]{:S(2)}, u32[]{:S(2)}) collective-permute-start(bf16[128,768]{1,0:T(8,128)(2,1)S(1)} %dynamic-slice_bitcast_fusion.12), channel_id=1, source_target_pairs={{0,4},{1,5},{2,6},{3,7},{4,0},{5,1},{6,2},{7,3},{8,12},{9,13},{10,... | collective-permute-start | bytes 589832 | tf_op jit(solution)/shard_map/ppermute | solution.py:295
  16.7 32.1 %collective-permute-start.25 = (bf16[96,768]{1,0:T(8,128)(2,1)}, bf16[96,768]{1,0:T(8,128)(2,1)S(1)}, u32[]{:S(2)}, u32[]{:S(2)}) collective-permute-start(bf16[96,768]{1,0:T(8,128)(2,1)} %param.25), channel_id=1, source_target_pairs={{0,4},{1,5},{2,6},{3,7},{4,0},{5,1},{6,2},{7,3},{8,12},{9,13},{10,... | collective-permute-start | bytes 442376 | tf_op jit(solution)/shard_map/ppermute | solution.py:295
  19.4 14.0 %collective-permute-start.7 = (bf16[2,2,1,288]{3,1,0,2:T(2,128)(2,1)S(1)}, bf16[2,2,1,288]{3,1,0,2:T(2,128)(2,1)S(1)}, u32[]{:S(2)}, u32[]{:S(2)}) collective-permute-start(bf16[2,2,1,288]{3,1,0,2:T(2,128)(2,1)S(1)} %pad_maximum_fusion.29), channel_id=1, source_target_pairs={{0,4},{1,5},{2,6},{3,7},{4,0},{5,1},{6,2},{7,3},{8,12},{9,13},{10,... | collective-permute-start | bytes 6920 | tf_op jit(solution)/shard_map/ppermute | solution.py:295
  38.5 12.0 %collective-permute-start.20 = (bf16[24,3072]{1,0:T(8,128)(2,1)S(1)}, bf16[24,3072]{1,0:T(8,128)(2,1)S(1)}, u32[]{:S(2)}, u32[]{:S(2)}) collective-permute-start(bf16[24,3072]{1,0:T(8,128)(2,1)S(1)} %copy-done.25), channel_id=1, source_target_pairs={{0,4},{1,5},{2,6},{3,7},{4,0},{5,1},{6,2},{7,3},{8,12},{9,13},{10,... | collective-permute-start | bytes 442376 | tf_op jit(solution)/shard_map/ppermute | solution.py:295
  43.7 11.0 %collective-permute-start.17 = (bf16[2,2,24,768]{3,2,1,0:T(8,128)(2,1)S(1)}, bf16[2,2,24,768]{3,2,1,0:T(8,128)(2,1)S(1)}, u32[]{:S(2)}, u32[]{:S(2)}) collective-permute-start(bf16[2,2,24,768]{3,2,1,0:T(8,128)(2,1)S(1)} %pad_maximum_fusion.23), channel_id=1, source_target_pairs={{0,2},{1,3},{2,0},{3,1},{4,6},{5,7},{6,4},{7,5},{8,10},{9,11},{10,... | collective-permute-start | bytes 442376 | tf_op jit(solution)/shard_map/ppermute | solution.py:295
  46.5 8.0 %collective-permute-start.12 = (bf16[2,2,24,576]{3,2,1,0:T(8,128)(2,1)S(1)}, bf16[2,2,24,576]{3,2,1,0:T(8,128)(2,1)S(1)}, u32[]{:S(2)}, u32[]{:S(2)}) collective-permute-start(bf16[2,2,24,576]{3,2,1,0:T(8,128)(2,1)S(1)} %pad_maximum_fusion.24), channel_id=1, source_target_pairs={{0,4},{1,5},{2,6},{3,7},{4,0},{5,1},{6,2},{7,3},{8,12},{9,13},{10,... | collective-permute-start | bytes 331784 | tf_op jit(solution)/shard_map/ppermute | solution.py:295
  48.9 15.1 %collective-permute-start.26 = (bf16[2,96,768]{2,1,0:T(8,128)(2,1)S(1)}, bf16[2,96,768]{2,1,0:T(8,128)(2,1)S(1)}, u32[]{:S(2)}, u32[]{:S(2)}) collective-permute-start(bf16[2,96,768]{2,1,0:T(8,128)(2,1)S(1)} %pad_maximum_fusion.20), channel_id=1, source_target_pairs={{0,16},{8,24},{16,0},{24,8},{1,17},{9,25},{17,1},{25,9},{2,18},{10... | collective-permute-start | bytes 884744 | tf_op jit(solution)/shard_map/ppermute | solution.py:295
  50.5 15.1 %collective-permute-start.21 = (bf16[2,24,3072]{2,1,0:T(8,128)(2,1)S(1)}, bf16[2,24,3072]{2,1,0:T(8,128)(2,1)S(1)}, u32[]{:S(2)}, u32[]{:S(2)}) collective-permute-start(bf16[2,24,3072]{2,1,0:T(8,128)(2,1)S(1)} %pad_maximum_fusion.19), channel_id=1, source_target_pairs={{0,2},{1,3},{2,0},{3,1},{4,6},{5,7},{6,4},{7,5},{8,10},{9,11},{10,... | collective-permute-start | bytes 884744 | tf_op jit(solution)/shard_map/ppermute | solution.py:295
  54.5 9.0 %collective-permute-start.1 = (bf16[2,128,384]{2,1,0:T(8,128)(2,1)S(1)}, bf16[2,128,384]{2,1,0:T(8,128)(2,1)S(1)}, u32[]{:S(2)}, u32[]{:S(2)}) collective-permute-start(bf16[2,128,384]{2,1,0:T(8,128)(2,1)S(1)} %get-tuple-element.69), channel_id=1, source_target_pairs={{0,2},{1,3},{2,0},{3,1},{4,6},{5,7},{6,4},{7,5},{8,10},{9,11},{10,... | collective-permute-start | bytes 589832 | tf_op jit(solution)/shard_map/ppermute | solution.py:295
  54.6 9.0 %collective-permute-start.13 = (bf16[2,2,2,24,576]{4,3,2,1,0:T(8,128)(2,1)S(1)}, bf16[2,2,2,24,576]{4,3,2,1,0:T(8,128)(2,1)S(1)}, u32[]{:S(2)}, u32[]{:S(2)}) collective-permute-start(bf16[2,2,2,24,576]{4,3,2,1,0:T(8,128)(2,1)S(1)} %pad_maximum_fusion.21), channel_id=1, source_target_pairs={{0,8},{8,0},{16,24},{24,16},{1,9},{9,1},{17,25},{25,17},{2,10},{10... | collective-permute-start | bytes 663560 | tf_op jit(solution)/shard_map/ppermute | solution.py:295
  57.3 9.9 %collective-permute-start.18 = (bf16[2,2,2,24,768]{4,3,2,1,0:T(8,128)(2,1)S(1)}, bf16[2,2,2,24,768]{4,3,2,1,0:T(8,128)(2,1)S(1)}, u32[]{:S(2)}, u32[]{:S(2)}) collective-permute-start(bf16[2,2,2,24,768]{4,3,2,1,0:T(8,128)(2,1)S(1)} %pad_maximum_fusion.18), channel_id=1, source_target_pairs={{0,16},{8,24},{16,0},{24,8},{1,17},{9,25},{17,1},{25,9},{2,18},{10... | collective-permute-start | bytes 884744 | tf_op jit(solution)/shard_map/ppermute | solution.py:295
  63.5 9.5 %collective-permute-start.4 = (bf16[2,2,128,384]{3,2,0,1:T(8,128)(2,1)S(1)}, bf16[2,2,128,384]{3,2,0,1:T(8,128)(2,1)S(1)}, u32[]{:S(2)}, u32[]{:S(2)}) collective-permute-start(bf16[2,2,128,384]{3,2,0,1:T(8,128)(2,1)S(1)} %pad_maximum_fusion.16), channel_id=1, source_target_pairs={{0,2},{1,3},{2,0},{3,1},{4,6},{5,7},{6,4},{7,5},{8,10},{9,11},{10,... | collective-permute-start | bytes 1179656 | tf_op jit(solution)/shard_map/ppermute | solution.py:295
  63.6 12.1 %collective-permute-start.2 = (bf16[2,2,128,384]{3,2,0,1:T(8,128)(2,1)S(1)}, bf16[2,2,128,384]{3,2,0,1:T(8,128)(2,1)S(1)}, u32[]{:S(2)}, u32[]{:S(2)}) collective-permute-start(bf16[2,2,128,384]{3,2,0,1:T(8,128)(2,1)S(1)} %pad_maximum_fusion.15), channel_id=1, source_target_pairs={{0,1},{1,0},{2,3},{3,2},{4,5},{5,4},{6,7},{7,6},{8,9},{9,8},{10,11... | collective-permute-start | bytes 1179656 | tf_op jit(solution)/shard_map/ppermute | solution.py:295
  64.0 27.4 %collective-permute-start.14 = (bf16[2,2,2,2,24,576]{5,4,3,2,1,0:T(8,128)(2,1)S(1)}, bf16[2,2,2,2,24,576]{5,4,3,2,1,0:T(8,128)(2,1)S(1)}, u32[]{:S(2)}, u32[]{:S(2)}) collective-permute-start(bf16[2,2,2,2,24,576]{5,4,3,2,1,0:T(8,128)(2,1)S(1)} %pad_maximum_fusion.14), channel_id=1, source_target_pairs={{0,16},{8,24},{16,0},{24,8},{1,17},{9,25},{17,1},{25,9},{2,18},{10... | collective-permute-start | bytes 1327112 | tf_op jit(solution)/shard_map/ppermute | solution.py:295
  65.7 20.2 %collective-permute-start.27 = (bf16[2,2,96,768]{3,2,1,0:T(8,128)(2,1)S(1)}, bf16[2,2,96,768]{3,2,1,0:T(8,128)(2,1)S(1)}, u32[]{:S(2)}, u32[]{:S(2)}) collective-permute-start(bf16[2,2,96,768]{3,2,1,0:T(8,128)(2,1)S(1)} %pad_maximum_fusion.13), channel_id=1, source_target_pairs={{0,1},{1,0},{2,3},{3,2},{4,5},{5,4},{6,7},{7,6},{8,9},{9,8},{10,11... | collective-permute-start | bytes 1769480 | tf_op jit(solution)/shard_map/ppermute | solution.py:295
  67.2 21.0 %collective-permute-start.22 = (bf16[2,2,24,3072]{3,2,1,0:T(8,128)(2,1)S(1)}, bf16[2,2,24,3072]{3,2,1,0:T(8,128)(2,1)S(1)}, u32[]{:S(2)}, u32[]{:S(2)}) collective-permute-start(bf16[2,2,24,3072]{3,2,1,0:T(8,128)(2,1)S(1)} %pad_maximum_fusion.12), channel_id=1, source_target_pairs={{0,16},{8,24},{16,0},{24,8},{1,17},{9,25},{17,1},{25,9},{2,18},{10... | collective-permute-start | bytes 1769480 | tf_op jit(solution)/shard_map/ppermute | solution.py:295
  73.0 59.8 %collective-permute-start.19 = (bf16[2,2,2,2,24,768]{5,4,3,2,1,0:T(8,128)(2,1)}, bf16[2,2,2,2,24,768]{5,4,3,2,1,0:T(8,128)(2,1)}, u32[]{:S(2)}, u32[]{:S(2)}) collective-permute-start(bf16[2,2,2,2,24,768]{5,4,3,2,1,0:T(8,128)(2,1)} %pad_maximum_fusion.11), channel_id=1, source_target_pairs={{0,8},{8,0},{16,24},{24,16},{1,9},{9,1},{17,25},{25,17},{2,10},{10... | collective-permute-start | bytes 1769480 | tf_op jit(solution)/shard_map/ppermute | solution.py:295
  86.0 25.5 %collective-permute-start.28 = (bf16[2,2,2,96,768]{4,3,2,1,0:T(8,128)(2,1)S(1)}, bf16[2,2,2,96,768]{4,3,2,1,0:T(8,128)(2,1)S(1)}, u32[]{:S(2)}, u32[]{:S(2)}) collective-permute-start(bf16[2,2,2,96,768]{4,3,2,1,0:T(8,128)(2,1)S(1)} %pad_maximum_fusion.7), channel_id=1, source_target_pairs={{0,2},{1,3},{2,0},{3,1},{4,6},{5,7},{6,4},{7,5},{8,10},{9,11},{10,... | collective-permute-start | bytes 3538952 | tf_op jit(solution)/shard_map/ppermute | solution.py:295
  88.4 26.3 %collective-permute-start.23 = (bf16[2,2,2,24,3072]{4,3,2,1,0:T(8,128)(2,1)S(1)}, bf16[2,2,2,24,3072]{4,3,2,1,0:T(8,128)(2,1)S(1)}, u32[]{:S(2)}, u32[]{:S(2)}) collective-permute-start(bf16[2,2,2,24,3072]{4,3,2,1,0:T(8,128)(2,1)S(1)} %pad_maximum_fusion.6), channel_id=1, source_target_pairs={{0,1},{1,0},{2,3},{3,2},{4,5},{5,4},{6,7},{7,6},{8,9},{9,8},{10,11... | collective-permute-start | bytes 3538952 | tf_op jit(solution)/shard_map/ppermute | solution.py:295
  113.5 31.9 %collective-permute-start.29 = (bf16[2,2,2,2,96,768]{5,4,3,2,1,0:T(8,128)(2,1)}, bf16[2,2,2,2,96,768]{5,4,3,2,1,0:T(8,128)(2,1)}, u32[]{:S(2)}, u32[]{:S(2)}) collective-permute-start(bf16[2,2,2,2,96,768]{5,4,3,2,1,0:T(8,128)(2,1)} %pad_maximum_fusion.3), channel_id=1, source_target_pairs={{0,8},{8,0},{16,24},{24,16},{1,9},{9,1},{17,25},{25,17},{2,10},{10... | collective-permute-start | bytes 7077896 | tf_op jit(solution)/shard_map/ppermute | solution.py:295
  117.1 30.9 %collective-permute-start.24 = (bf16[2,2,2,2,24,3072]{5,4,3,2,1,0:T(8,128)(2,1)}, bf16[2,2,2,2,24,3072]{5,4,3,2,1,0:T(8,128)(2,1)}, u32[]{:S(2)}, u32[]{:S(2)}) collective-permute-start(bf16[2,2,2,2,24,3072]{5,4,3,2,1,0:T(8,128)(2,1)} %pad_maximum_fusion.2), channel_id=1, source_target_pairs={{0,8},{8,0},{16,24},{24,16},{1,9},{9,1},{17,25},{25,17},{2,10},{10... | collective-permute-start | bytes 7077896 | tf_op jit(solution)/shard_map/ppermute | solution.py:295
  126.0 17.0 %all-to-all-start = ((bf16[8,128,192]{1,2,0:T(8,128)(2,1)}), bf16[8,128,192]{1,2,0:T(8,128)(2,1)S(1)}, u32[]{:S(2)}, u32[]{:S(2)}) async-start(bf16[8,128,192]{1,2,0:T(8,128)(2,1)} %copy.83), calls=%async_computation | async-start | bytes 786432 | tf_op jit(solution)/shard_map/all_to_all | solution.py:535
  174.1 24.8 %all-to-all-start.1 = ((bf16[8,128,192]{1,2,0:T(8,128)(2,1)}), bf16[8,128,192]{1,2,0:T(8,128)(2,1)}, u32[]{:S(2)}, u32[]{:S(2)}) async-start(bf16[8,128,192]{1,2,0:T(8,128)(2,1)} %bitcast.96), calls=%async_computation.1 | async-start | bytes 786432 | tf_op jit(solution)/shard_map/all_to_all | solution.py:544
  178.6 17.6 %collective-permute-start.45 = (bf16[2,2,2,2,24,768]{5,4,1,2,3,0:T(8,128)(2,1)S(1)}, bf16[2,2,2,2,24,768]{5,4,1,2,3,0:T(8,128)(2,1)S(1)}, u32[]{:S(2)}, u32[]{:S(2)}) collective-permute-start(bf16[2,2,2,2,24,768]{5,4,1,2,3,0:T(8,128)(2,1)S(1)} %bitcast.480), channel_id=1, source_target_pairs={{0,8},{8,0},{16,24},{24,16},{1,9},{9,1},{17,25},{25,17},{2,10},{10... | collective-permute-start | bytes 1769480 | tf_op jit(solution)/shard_map/ppermute | solution.py:295
  189.9 92.7 %collective-permute-start.50 = (bf16[2,2,2,2,24,3072]{5,4,1,3,0,2:T(8,128)(2,1)}, bf16[2,2,2,2,24,3072]{5,4,1,3,0,2:T(8,128)(2,1)}, u32[]{:S(2)}, u32[]{:S(2)}) collective-permute-start(bf16[2,2,2,2,24,3072]{5,4,1,3,0,2:T(8,128)(2,1)} %bitcast.440), channel_id=1, source_target_pairs={{0,8},{8,0},{16,24},{24,16},{1,9},{9,1},{17,25},{25,17},{2,10},{10... | collective-permute-start | bytes 7077896 | tf_op jit(solution)/shard_map/ppermute | solution.py:295
  196.1 93.0 %collective-permute-start.55 = (bf16[2,2,2,2,96,768]{5,4,1,0,2,3:T(8,128)(2,1)}, bf16[2,2,2,2,96,768]{5,4,1,0,2,3:T(8,128)(2,1)}, u32[]{:S(2)}, u32[]{:S(2)}) collective-permute-start(bf16[2,2,2,2,96,768]{5,4,1,0,2,3:T(8,128)(2,1)} %bitcast.439), channel_id=1, source_target_pairs={{0,8},{8,0},{16,24},{24,16},{1,9},{9,1},{17,25},{25,17},{2,10},{10... | collective-permute-start | bytes 7077896 | tf_op jit(solution)/shard_map/ppermute | solution.py:295
  197.8 42.3 %collective-permute-start.46 = (bf16[2,2,2,24,768]{4,3,0,1,2:T(8,128)(2,1)}, bf16[2,2,2,24,768]{4,3,0,1,2:T(8,128)(2,1)}, u32[]{:S(2)}, u32[]{:S(2)}) collective-permute-start(bf16[2,2,2,24,768]{4,3,0,1,2:T(8,128)(2,1)} %dynamic-slice_bitcast_fusion.8), channel_id=1, source_target_pairs={{0,16},{8,24},{16,0},{24,8},{1,17},{9,25},{17,1},{25,9},{2,18},{10... | collective-permute-start | bytes 884744 | tf_op jit(solution)/shard_map/ppermute | solution.py:295
  226.2 21.8 %collective-permute-start.30 = (bf16[2,2,128,384]{3,2,0,1:T(8,128)(2,1)S(1)}, bf16[2,2,128,384]{3,2,0,1:T(8,128)(2,1)}, u32[]{:S(2)}, u32[]{:S(2)}) collective-permute-start(bf16[2,2,128,384]{3,2,0,1:T(8,128)(2,1)S(1)} %bitcast.481), channel_id=1, source_target_pairs={{0,2},{1,3},{2,0},{3,1},{4,6},{5,7},{6,4},{7,5},{8,10},{9,11},{10,... | collective-permute-start | bytes 1179656 | tf_op jit(solution)/shard_map/ppermute | solution.py:295
  237.0 14.6 %collective-permute-start.32 = (bf16[2,2,128,384]{3,2,1,0:T(8,128)(2,1)S(1)}, bf16[2,2,128,384]{3,2,1,0:T(8,128)(2,1)S(1)}, u32[]{:S(2)}, u32[]{:S(2)}) collective-permute-start(bf16[2,2,128,384]{3,2,1,0:T(8,128)(2,1)S(1)} %dynamic-slice_bitcast_fusion.5), channel_id=1, source_target_pairs={{0,1},{1,0},{2,3},{3,2},{4,5},{5,4},{6,7},{7,6},{8,9},{9,8},{10,11... | collective-permute-start | bytes 1179656 | tf_op jit(solution)/shard_map/ppermute | solution.py:295
  241.2 6.8 %collective-permute-start.47 = (bf16[2,2,24,768]{3,2,0,1:T(8,128)(2,1)S(1)}, bf16[2,2,24,768]{3,2,0,1:T(8,128)(2,1)S(1)}, u32[]{:S(2)}, u32[]{:S(2)}) collective-permute-start(bf16[2,2,24,768]{3,2,0,1:T(8,128)(2,1)S(1)} %dynamic-slice_bitcast_fusion.15), channel_id=1, source_target_pairs={{0,1},{1,0},{2,3},{3,2},{4,5},{5,4},{6,7},{7,6},{8,9},{9,8},{10,11... | collective-permute-start | bytes 442376 | tf_op jit(solution)/shard_map/ppermute | solution.py:295
  247.9 7.3 %collective-permute-start.40 = (bf16[2,2,2,2,24,576]{5,4,3,2,1,0:T(8,128)(2,1)S(1)}, bf16[2,2,2,2,24,576]{5,4,3,2,1,0:T(8,128)(2,1)S(1)}, u32[]{:S(2)}, u32[]{:S(2)}) collective-permute-start(bf16[2,2,2,2,24,576]{5,4,3,2,1,0:T(8,128)(2,1)S(1)} %dynamic-slice_bitcast_fusion.4), channel_id=1, source_target_pairs={{0,8},{8,0},{16,24},{24,16},{1,9},{9,1},{17,25},{25,17},{2,10},{10... | collective-permute-start | bytes 1327112 | tf_op jit(solution)/shard_map/ppermute | solution.py:295
  251.6 10.2 %collective-permute-start.31 = (bf16[2,128,384]{2,1,0:T(8,128)(2,1)S(1)}, bf16[2,128,384]{2,1,0:T(8,128)(2,1)S(1)}, u32[]{:S(2)}, u32[]{:S(2)}) collective-permute-start(bf16[2,128,384]{2,1,0:T(8,128)(2,1)S(1)} %dynamic-slice_bitcast_fusion.11), channel_id=1, source_target_pairs={{0,1},{1,0},{2,3},{3,2},{4,5},{5,4},{6,7},{7,6},{8,9},{9,8},{10,11... | collective-permute-start | bytes 589832 | tf_op jit(solution)/shard_map/ppermute | solution.py:295
  253.4 8.5 %collective-permute-start.33 = (bf16[2,128,384]{2,1,0:T(8,128)(2,1)S(1)}, bf16[2,128,384]{2,1,0:T(8,128)(2,1)S(1)}, u32[]{:S(2)}, u32[]{:S(2)}) collective-permute-start(bf16[2,128,384]{2,1,0:T(8,128)(2,1)S(1)} %dynamic-slice_bitcast_fusion.10), channel_id=1, source_target_pairs={{0,2},{1,3},{2,0},{3,1},{4,6},{5,7},{6,4},{7,5},{8,10},{9,11},{10,... | collective-permute-start | bytes 589832 | tf_op jit(solution)/shard_map/ppermute | solution.py:295
  266.8 12.5 %collective-permute-start.42 = (bf16[2,2,24,576]{3,2,1,0:T(8,128)(2,1)S(1)}, bf16[2,2,24,576]{3,2,1,0:T(8,128)(2,1)S(1)}, u32[]{:S(2)}, u32[]{:S(2)}) collective-permute-start(bf16[2,2,24,576]{3,2,1,0:T(8,128)(2,1)S(1)} %dynamic-slice_bitcast_fusion.16), channel_id=1, source_target_pairs={{0,4},{1,5},{2,6},{3,7},{4,0},{5,1},{6,2},{7,3},{8,12},{9,13},{10,... | collective-permute-start | bytes 331784 | tf_op jit(solution)/shard_map/ppermute | solution.py:295
  270.0 12.2 %collective-permute-start.34 = (bf16[128,768]{1,0:T(8,128)(2,1)S(1)}, bf16[128,768]{1,0:T(8,128)(2,1)S(1)}, u32[]{:S(2)}, u32[]{:S(2)}) collective-permute-start(bf16[128,768]{1,0:T(8,128)(2,1)S(1)} %fusion.47), channel_id=1, source_target_pairs={{0,4},{1,5},{2,6},{3,7},{4,0},{5,1},{6,2},{7,3},{8,12},{9,13},{10,... | collective-permute-start | bytes 589832 | tf_op jit(solution)/shard_map/ppermute | solution.py:295
  279.4 8.1 %collective-permute-start.43 = (bf16[2,24,576]{2,1,0:T(8,128)(2,1)S(1)}, bf16[2,24,576]{2,1,0:T(8,128)(2,1)S(1)}, u32[]{:S(2)}, u32[]{:S(2)}) collective-permute-start(bf16[2,24,576]{2,1,0:T(8,128)(2,1)S(1)} %dynamic-slice_bitcast_fusion.18), channel_id=1, source_target_pairs={{0,2},{1,3},{2,0},{3,1},{4,6},{5,7},{6,4},{7,5},{8,10},{9,11},{10,... | collective-permute-start | bytes 165896 | tf_op jit(solution)/shard_map/ppermute | solution.py:295
  285.3 26.7 %collective-permute-start.51 = (bf16[2,2,2,24,3072]{4,3,1,2,0:T(8,128)(2,1)S(1)}, bf16[2,2,2,24,3072]{4,3,1,2,0:T(8,128)(2,1)S(1)}, u32[]{:S(2)}, u32[]{:S(2)}) collective-permute-start(bf16[2,2,2,24,3072]{4,3,1,2,0:T(8,128)(2,1)S(1)} %dynamic-slice_bitcast_fusion.1), channel_id=1, source_target_pairs={{0,2},{1,3},{2,0},{3,1},{4,6},{5,7},{6,4},{7,5},{8,10},{9,11},{10,... | collective-permute-start | bytes 3538952 | tf_op jit(solution)/shard_map/ppermute | solution.py:295
  287.6 27.6 %collective-permute-start.44 = (bf16[2,24,576]{2,1,0:T(8,128)(2,1)S(1)}, bf16[2,24,576]{2,1,0:T(8,128)(2,1)S(1)}, u32[]{:S(2)}, u32[]{:S(2)}) collective-permute-start(bf16[2,24,576]{2,1,0:T(8,128)(2,1)S(1)} %fusion.57), channel_id=1, source_target_pairs={{0,1},{1,0},{2,3},{3,2},{4,5},{5,4},{6,7},{7,6},{8,9},{9,8},{10,11... | collective-permute-start | bytes 165896 | tf_op jit(solution)/shard_map/ppermute | solution.py:295
  292.6 26.7 %collective-permute-start.56 = (bf16[2,2,2,96,768]{4,3,1,0,2:T(8,128)(2,1)}, bf16[2,2,2,96,768]{4,3,1,0,2:T(8,128)(2,1)}, u32[]{:S(2)}, u32[]{:S(2)}) collective-permute-start(bf16[2,2,2,96,768]{4,3,1,0,2:T(8,128)(2,1)} %dynamic-slice_bitcast_fusion), channel_id=1, source_target_pairs={{0,1},{1,0},{2,3},{3,2},{4,5},{5,4},{6,7},{7,6},{8,9},{9,8},{10,11... | collective-permute-start | bytes 3538952 | tf_op jit(solution)/shard_map/ppermute | solution.py:295
  314.3 13.5 %collective-permute-start.52 = (bf16[2,2,24,3072]{3,2,0,1:T(8,128)(2,1)}, bf16[2,2,24,3072]{3,2,0,1:T(8,128)(2,1)}, u32[]{:S(2)}, u32[]{:S(2)}) collective-permute-start(bf16[2,2,24,3072]{3,2,0,1:T(8,128)(2,1)} %dynamic-slice_bitcast_fusion.3), channel_id=1, source_target_pairs={{0,16},{8,24},{16,0},{24,8},{1,17},{9,25},{17,1},{25,9},{2,18},{10... | collective-permute-start | bytes 1769480 | tf_op jit(solution)/shard_map/ppermute | solution.py:295
  320.9 12.8 %collective-permute-start.57 = (bf16[2,2,96,768]{3,2,1,0:T(8,128)(2,1)S(1)}, bf16[2,2,96,768]{3,2,1,0:T(8,128)(2,1)S(1)}, u32[]{:S(2)}, u32[]{:S(2)}) collective-permute-start(bf16[2,2,96,768]{3,2,1,0:T(8,128)(2,1)S(1)} %dynamic-slice_bitcast_fusion.2), channel_id=1, source_target_pairs={{0,2},{1,3},{2,0},{3,1},{4,6},{5,7},{6,4},{7,5},{8,10},{9,11},{10,... | collective-permute-start | bytes 1769480 | tf_op jit(solution)/shard_map/ppermute | solution.py:295
  329.0 6.8 %collective-permute-start.53 = (bf16[2,24,3072]{2,1,0:T(8,128)(2,1)S(1)}, bf16[2,24,3072]{2,1,0:T(8,128)(2,1)S(1)}, u32[]{:S(2)}, u32[]{:S(2)}) collective-permute-start(bf16[2,24,3072]{2,1,0:T(8,128)(2,1)S(1)} %dynamic-slice_bitcast_fusion.7), channel_id=1, source_target_pairs={{0,1},{1,0},{2,3},{3,2},{4,5},{5,4},{6,7},{7,6},{8,9},{9,8},{10,11... | collective-permute-start | bytes 884744 | tf_op jit(solution)/shard_map/ppermute | solution.py:295
  333.9 6.8 %collective-permute-start.58 = (bf16[2,96,768]{2,1,0:T(8,128)(2,1)S(1)}, bf16[2,96,768]{2,1,0:T(8,128)(2,1)S(1)}, u32[]{:S(2)}, u32[]{:S(2)}) collective-permute-start(bf16[2,96,768]{2,1,0:T(8,128)(2,1)S(1)} %dynamic-slice_bitcast_fusion.6), channel_id=1, source_target_pairs={{0,16},{8,24},{16,0},{24,8},{1,17},{9,25},{17,1},{25,9},{2,18},{10... | collective-permute-start | bytes 884744 | tf_op jit(solution)/shard_map/ppermute | solution.py:295
  335.9 11.6 %collective-permute-start.54 = (bf16[24,3072]{1,0:T(8,128)(2,1)S(1)}, bf16[24,3072]{1,0:T(8,128)(2,1)S(1)}, u32[]{:S(2)}, u32[]{:S(2)}) collective-permute-start(bf16[24,3072]{1,0:T(8,128)(2,1)S(1)} %dynamic-slice_bitcast_fusion.14), channel_id=1, source_target_pairs={{0,4},{1,5},{2,6},{3,7},{4,0},{5,1},{6,2},{7,3},{8,12},{9,13},{10,... | collective-permute-start | bytes 442376 | tf_op jit(solution)/shard_map/ppermute | solution.py:295
  340.8 8.3 %collective-permute-start.59 = (bf16[96,768]{1,0:T(8,128)(2,1)S(1)}, bf16[96,768]{1,0:T(8,128)(2,1)S(1)}, u32[]{:S(2)}, u32[]{:S(2)}) collective-permute-start(bf16[96,768]{1,0:T(8,128)(2,1)S(1)} %dynamic-slice_bitcast_fusion.13), channel_id=1, source_target_pairs={{0,4},{1,5},{2,6},{3,7},{4,0},{5,1},{6,2},{7,3},{8,12},{9,13},{10,... | collective-permute-start | bytes 442376 | tf_op jit(solution)/shard_map/ppermute | solution.py:295
  (57 other events, 757.7 us)
